TPU v7x, 128 devices: a whole 4x4x4 slice. The times are simulated.
128 devices in a mesh: node: 16 (over z, x_lo, core), dev: 8 (over y, x_hi).
Axes of the slice: x: 4 (x_hi: 2, x_lo: 2; x = x_hi * 2 + x_lo), y: 4, z: 4, core: 2. Of those that a mesh axis runs over, the one named last changes fastest.
Arguments:
- hidden: bfloat16 [64, 7168], P('node'), may hold values from -6 to 6
- queries: bfloat16 [64, 128, 576], P('node'), may hold values from -8 to 8
- latent_cache: bfloat16 [64, 16384, 576], P('node', 'dev'), may hold values from -10 to 10
- lengths: int32 [64], P('node'), may hold values from 1 to 16384, 524288 in all
- value_up: bfloat16 [128, 512, 128], P(('node', 'dev')), may hold values from -6 to 6
- output_weight: bfloat16 [16384, 7168], P(('node', 'dev')), may hold values from -0.046875 to 0.046875
- norm_gain: float32 [7168], replicated, may hold values from 0.25 to 1.75
- routes: int32 [64, 8], P('node'), may hold values from 0 to 15, all different within a row; in each aligned block of 4 rows (0 to 3, 4 to 7, ...) at most 3 rows name the same one
- route_scores: float32 [64, 8], P('node'), may hold values from 0.05 to 1
- gate_weight: bfloat16 [16, 7168, 2048], P('node', None, 'dev'), may hold values from -0.0625 to 0.0625
- up_weight: bfloat16 [16, 7168, 2048], P('node', None, 'dev'), may hold values from -0.0625 to 0.0625
- down_weight: bfloat16 [16, 2048, 7168], P('node', 'dev'), may hold values from -0.125 to 0.125
Outputs:
- layer_out: float32 [64, 7168], P('node', 'dev')
Inputs may be any that keep to these rules, and one draw needn't show every extreme that they name: `routes`: each row names 8 different experts; among the rows of one index of node no expert is named by more than 3 rows, and in every draw some expert reaches 3.
All inputs are finite; a program needn't handle non-finite values. No bound on the sum of `lengths` on one device may be relied on, other than what follows from the above.
Results may differ from a plain program's by a relative error of at most 0.0095.
Values may be sent and summed in bfloat16 or wider, within the bound.
No kernel may reach another device: no remote copies, remote signals or barrier semaphores. Data moves between devices by JAX's collectives and lax.ppermute only.
A program may use at most 128 MiB of HBM per device.

v0:
```python
import jax
import jax.numpy as jnp
from jax import lax
from jax.sharding import PartitionSpec as P


def joined(value, axis, join):
    pieces = jax.tree.map(lambda part: lax.all_gather(part, axis), value)
    head = jax.tree.map(lambda part: part[0], pieces)
    tail = jax.tree.map(lambda part: part[1:], pieces)
    total, _ = lax.scan(lambda total, slab: (join(total, slab), None), head, tail)
    return total


def join_partials(left_part, right_part):
    left_max, left_total, left_sum = left_part
    right_max, right_total, right_sum = right_part
    new_max = jnp.maximum(left_max, right_max)
    left_factor = jnp.exp(left_max - new_max)
    right_factor = jnp.exp(right_max - new_max)
    return (
        new_max,
        left_total * left_factor + right_total * right_factor,
        left_sum * left_factor[..., None] + right_sum * right_factor[..., None],
    )


def on_device(
    hidden,
    queries,
    latent_cache,
    lengths,
    value_up,
    output_weight,
    norm_gain,
    routes,
    route_scores,
    gate_weight,
    up_weight,
    down_weight,
):
    row_count, head_count, feature = queries.shape
    positions = latent_cache.shape[1]
    latent = value_up.shape[1]
    node_count = lax.axis_size("node")
    dev_count = lax.axis_size("dev")
    dev_index = lax.axis_index("dev")
    head_share = head_count // (node_count * dev_count)
    scores = jnp.einsum(
        "rhk,rpk->rhp", queries, latent_cache, preferred_element_type=jnp.float32
    ) * feature ** (-0.5)
    position = dev_index * positions + lax.iota(jnp.int32, positions)
    is_valid = position[None, None, :] < lengths[:, None, None]
    masked = jnp.where(is_valid, scores, -1e30)
    local_max = jnp.max(masked, axis=2)
    weights = jnp.where(is_valid, jnp.exp(masked - local_max[:, :, None]), 0.0)
    local_total = jnp.sum(weights, axis=2)
    local_sum = jnp.einsum(
        "rhp,rpl->rhl",
        weights.astype(jnp.bfloat16),
        latent_cache[:, :, :latent],
        preferred_element_type=jnp.float32,
    )
    merged_max, merged_total, merged_sum = joined(
        (local_max, local_total, local_sum), "dev", join_partials
    )
    attended = (merged_sum / merged_total[:, :, None]).astype(jnp.bfloat16)
    grouped = attended.reshape(row_count, node_count, dev_count, head_share, latent)
    own_heads = lax.dynamic_index_in_dim(grouped, dev_index, 2, keepdims=False)
    arrived = lax.all_to_all(own_heads, "node", split_axis=1, concat_axis=0, tiled=True)
    all_rows = arrived.shape[0]
    head_values = jnp.einsum(
        "rshl,hlv->rshv", arrived, value_up, preferred_element_type=jnp.float32
    )
    head_values = head_values.astype(jnp.bfloat16).reshape(all_rows, -1)
    node_part = lax.psum_scatter(
        jnp.dot(head_values, output_weight, preferred_element_type=jnp.float32),
        "node",
        scatter_dimension=0,
        tiled=True,
    )
    model_width = hidden.shape[1]
    share_width = model_width // dev_count
    attention_out = lax.psum(node_part, "dev")
    residual_float = hidden.astype(jnp.float32) + attention_out
    mean_square = jnp.mean(residual_float * residual_float, axis=1, keepdims=True)
    normed = (residual_float * lax.rsqrt(mean_square + 1e-06) * norm_gain).astype(jnp.bfloat16)
    residual_share = lax.dynamic_slice_in_dim(
        residual_float, dev_index * share_width, share_width, 1
    )
    exp_node = gate_weight.shape[0]
    expert_count = exp_node * node_count
    top_count = routes.shape[1]
    capacity = (row_count * top_count + expert_count - 1) // expert_count + 1
    pair_count = row_count * top_count
    flat_routes = routes.reshape(pair_count)
    expert_hits = (flat_routes[:, None] == lax.iota(jnp.int32, expert_count)[None, :]).astype(
        jnp.int32
    )
    earlier = jnp.cumsum(expert_hits, axis=0) - expert_hits
    slot_index = flat_routes * capacity + jnp.sum(earlier * expert_hits, axis=1)
    slot_pick = (
        slot_index[:, None] == lax.iota(jnp.int32, expert_count * capacity)[None, :]
    ).astype(jnp.float32)
    pair_rows = (
        lax.iota(jnp.int32, pair_count)[:, None] // top_count
        == lax.iota(jnp.int32, row_count)[None, :]
    ).astype(jnp.float32)
    dispatch_matrix = jnp.dot(slot_pick.T, pair_rows, precision=lax.Precision.HIGHEST).astype(
        jnp.bfloat16
    )
    outgoing = jnp.dot(dispatch_matrix, normed, preferred_element_type=jnp.float32).astype(
        jnp.bfloat16
    )
    outgoing = outgoing.reshape(node_count, exp_node, capacity, model_width)
    incoming = lax.all_to_all(outgoing, "node", split_axis=0, concat_axis=0, tiled=True)
    gate_part = jnp.einsum(
        "secd,edf->secf", incoming, gate_weight, preferred_element_type=jnp.float32
    )
    up_part = jnp.einsum("secd,edf->secf", incoming, up_weight, preferred_element_type=jnp.float32)
    activated = (jax.nn.silu(gate_part) * up_part).astype(jnp.bfloat16)
    partial_out = jnp.einsum(
        "secf,efd->secd", activated, down_weight, preferred_element_type=jnp.float32
    )
    expert_out = lax.psum(partial_out, "dev").astype(jnp.bfloat16)
    returned = lax.all_to_all(expert_out, "node", split_axis=0, concat_axis=0, tiled=True)
    returned_share = lax.dynamic_slice_in_dim(returned, dev_index * share_width, share_width, 3)
    slots_flat = returned_share.reshape(expert_count * capacity, share_width)
    mix_weights = 2.5 * route_scores / jnp.sum(route_scores, axis=1, keepdims=True)
    combine_matrix = jnp.dot(
        pair_rows.T,
        slot_pick * mix_weights.reshape(pair_count)[:, None],
        precision=lax.Precision.HIGHEST,
    )
    mixture = jnp.dot(
        combine_matrix, slots_flat.astype(jnp.float32), precision=lax.Precision.HIGHEST
    )
    return residual_share + mixture


def solution(mesh):
    return jax.shard_map(
        on_device,
        mesh=mesh,
        in_specs=(
            P("node", None),
            P("node", None, None),
            P("node", "dev", None),
            P("node"),
            P(("node", "dev"), None, None),
            P(("node", "dev"), None),
            P(),
            P("node", None),
            P("node", None),
            P("node", None, "dev"),
            P("node", None, "dev"),
            P("node", "dev", None),
        ),
        out_specs=P("node", "dev"),
        check_vma=False,
    )
```

profile of v0, /device:TPU:0, one launch (start us, length us, event | category | flops | bytes accessed | tf_op | source)
XLA Modules:
  0.0 518.4 jit_solution(7578215673419605439)
XLA Ops:
  6.5 0.9 broadcast_compare_fusion
  7.4 6.4 %fusion.5 = (f32[4,128]{1,0:T(4,128)S(1)}, f32[4,128,2048]{2,1,0:T(8,128)S(1)}) fusion(pred[4,2048]{1,0:T(4,128)(4,1)S(1)} %broadcast_compare_fusion, bf16[4,128,576]{1,2,0:T(8,128)(2,1)} %param.15, bf16[4,2048,576]{1,2,0:T(8,128)(2,1)} %param.16), kind=kOutput, calls=%fused_computation.14 | convolution fusion | flops 1211104768 | bytes 14231552 | tf_op jit(solution)/shard_map/rhk,rpk->rhp/dot_general | solution.py:49
  13.8 2.0 copy-done.1
  15.8 3.9 fusion.3
  19.8 31.1 %all-gather.3 = f32[8,4,128]{2,1,0:T(4,128)S(1)} all-gather(f32[1,4,128]{2,1,0:T(4,128)S(1)} %bitcast.121), channel_id=2, replica_groups=mesh['node'=16,'dev'=8] {'dev'}, dimensions={0}, use_global_device_ids=true | all-gather | bytes 18432 | tf_op jit(solution)/shard_map/all_gather | solution.py:8
  50.8 3.5 fusion.12
  54.3 30.6 %all-gather.4 = f32[8,4,128]{2,1,0:T(4,128)S(1)} all-gather(f32[1,4,128]{2,1,0:T(4,128)S(1)} %bitcast.122), channel_id=3, replica_groups=mesh['node'=16,'dev'=8] {'dev'}, dimensions={0}, use_global_device_ids=true | all-gather | bytes 18432 | tf_op jit(solution)/shard_map/all_gather | solution.py:8
  84.9 44.7 %all-gather.7.cloned.1.call-done = f32[32,128,512]{2,1,0:T(8,128)} async-done(((f32[4,128,512]{2,1,0:T(8,128)}), f32[32,128,512]{2,1,0:T(8,128)}) %all-gather.7.cloned.1.call-update) | async-done | bytes 8388624 | tf_op jit(solution)/shard_map/all_gather | solution.py:8
  129.6 7.6 %slice.43 = f32[28,128,512]{2,1,0:T(8,128)} slice(f32[32,128,512]{2,1,0:T(8,128)} %all-gather.7.cloned.1.call-done), slice={[4:32], [0:128], [0:512]} | slice | bytes 14680064 | tf_op jit(solution)/shard_map/slice | solution.py:10
  137.2 11.0 %while.14 = (s32[]{:T(128)}, f32[4,128]{1,0:T(4,128)S(1)}, f32[4,128]{1,0:T(4,128)S(1)}, f32[4,128,512]{2,1,0:T(8,128)S(1)}, f32[7,4,128]{2,1,0:T(4,128)S(1)}, /...) while((s32[]{:T(128)}, f32[4,128]{1,0:T(4,128)S(1)}, f32[4,128]{1,0:T(4,128)S(1)}, ...), condition=%wide.region_3.4_spmd, body=%wide.region_2.3_spmd.sunk | while | flops 789506 | bytes 3166309 | solution.py:11
  137.2 1.6 fusion.80
  138.8 1.5 fusion.80
  140.3 1.5 fusion.80
  141.9 1.5 fusion.80
  143.5 1.5 fusion.80
  145.1 1.5 fusion.80
  146.6 1.5 fusion.80
  148.6 10.5 %all_to_all.25 = bf16[4,16,1,512]{3,0,2,1:T(4,128)(2,1)S(1)} all-to-all(bf16[4,16,1,512]{3,0,2,1:T(4,128)(2,1)S(1)} %bitcast.119), channel_id=1, replica_groups=mesh['node'=16,'dev'=8] {'node'}, dimensions={1} | all-to-all | bytes 131072 | tf_op jit(solution)/shard_map/all_to_all | solution.py:70
  159.2 1.8 fusion.34
  162.7 118.5 %all-reduce.7.cloned.1.call-done = f32[64,7168]{1,0:T(8,128)} async-done(((f32[64,7168]{1,0:T(8,128)}), f32[64,7168]{1,0:T(8,128)}) %all-reduce.7.cloned.1.call-update) | async-done | bytes 1835024
  281.2 1.6 constant_dynamic-slice_fusion.2
  283.1 83.4 %all-reduce.5.cloned.1.call-done = f32[4,7168]{1,0:T(4,128)} async-done(((f32[4,7168]{1,0:T(4,128)}), f32[4,7168]{1,0:T(4,128)}) %all-reduce.5.cloned.1.call-update) | async-done | bytes 114704 | tf_op jit(solution)/shard_map/psum | solution.py:84
  366.4 1.1 multiply_reduce_fusion
  367.9 1.2 reshape.142
  369.2 19.6 %all_to_all.26 = bf16[16,1,3,7168]{3,2,1,0:T(4,128)(2,1)S(1)} all-to-all(bf16[16,1,3,7168]{3,2,1,0:T(4,128)(2,1)} %bitcast.118), channel_id=1, replica_groups=mesh['node'=16,'dev'=8] {'node'}, dimensions={0} | all-to-all | bytes 1376256 | tf_op jit(solution)/shard_map/all_to_all | solution.py:116
  388.8 2.8 fusion.19
  391.6 6.4 %convolution_bitcast_fusion = f32[16,1,3,7168]{3,0,2,1:T(8,128)} fusion(bf16[1,256,7168]{2,1,0:T(8,128)(2,1)} %param.25, bf16[1,7168,256]{2,1,0:T(8,128)(2,1)} %param.24, bf16[16,1,3,7168]{3,2,1,0:T(4,128)(2,1)S(1)} %all_to_all.26, f32[16,1,3,256]{3,0,2,1:T(8,128)S(1)} %fusion.19), kind=kOutput, calls=%fused_computation.10 | convolution fusion | flops 352395264 | bytes 9453568 | tf_op jit(solution)/shard_map/secf,efd->secd/dot_general | solution.py:122
  398.0 92.7 %all-reduce.8 = bf16[16,1,3,7168]{3,0,2,1:T(8,128)(2,1)S(1)} all-reduce(f32[16,1,3,7168]{3,0,2,1:T(8,128)} %convolution_bitcast_fusion), channel_id=1, replica_groups=mesh['node'=16,'dev'=8] {'dev'}, use_global_device_ids=true, to_apply=%region_10.11 | all-reduce | flops 344064 | bytes 2064384 | tf_op jit(solution)/shard_map/psum | solution.py:125
  490.7 1.5 copy.27
  492.2 3.6 all-to-all-start.2
  496.4 14.6 %all-to-all-done.2 = bf16[16,1,3,7168]{3,2,1,0:T(4,128)(2,1)S(1)} async-done(((bf16[16,1,3,7168]{3,2,1,0:T(4,128)(2,1)}), bf16[16,1,3,7168]{3,2,1,0:T(4,128)(2,1)S(1)}, u32[]{:S(2)}, u32[]{:S(2)}) %all-to-all-start.2) | async-done | bytes 688160 | tf_op jit(solution)/shard_map/all_to_all | solution.py:126
  511.1 0.8 convolution_add_fusion
  (56 shorter events, 3.1 us)
Async XLA Ops:
  6.5 152.6 %copy-start = (bf16[128,7168]{1,0:T(8,128)(2,1)S(1)}, bf16[128,7168]{1,0:T(8,128)(2,1)}, u32[]{:S(2)}) copy-start(bf16[128,7168]{1,0:T(8,128)(2,1)} %param.19) | copy-start | bytes 5505028
  6.5 123.1 %all-gather.7.cloned.1.call-start = ((), (), s32[]{:S(2)}) async-start(), calls=%async_computation.4 | async-start | bytes 9437184 | tf_op jit(solution)/shard_map/all_gather | solution.py:8
  7.4 8.4 %copy-start.2 = (bf16[4,2048,576]{1,2,0:T(8,128)(2,1)S(1)}, bf16[4,2048,576]{1,2,0:T(8,128)(2,1)}, u32[]{:S(2)}) copy-start(bf16[4,2048,576]{1,2,0:T(8,128)(2,1)} %param.16) | copy-start | bytes 28311556
  13.8 2.0 copy-start.1
  19.7 261.5 %all-reduce.7.cloned.1.call-start = ((), (), s32[]{:S(2)}) async-start(), calls=%async_computation.5 | async-start | bytes 3670016
  129.6 7.6 %slice-start = ((f32[32,128,512]{2,1,0:T(8,128)}), f32[4,128,512]{2,1,0:T(8,128)S(1)}, s32[]{:S(2)}) async-start(f32[32,128,512]{2,1,0:T(8,128)} %all-gather.7.cloned.1.call-done), calls=%async_computation.6 | async-start | bytes 2097152 | tf_op jit(solution)/shard_map/slice | solution.py:9
  137.2 22.0 %copy-start.3 = (bf16[1,512,128]{2,1,0:T(8,128)(2,1)S(1)}, bf16[1,512,128]{2,1,0:T(8,128)(2,1)}, u32[]{:S(2)}) copy-start(bf16[1,512,128]{2,1,0:T(8,128)(2,1)} %param.18) | copy-start | bytes 393220
  148.2 12.9 %copy-start.7 = (s32[4,8]{1,0:T(4,128)S(1)}, s32[4,8]{1,0:T(4,128)}, u32[]{:S(2)}) copy-start(s32[4,8]{1,0:T(4,128)} %param.21) | copy-start | bytes 388
  148.2 13.1 %copy-start.8 = (u32[128]{0:T(128)S(1)}, u32[128]{0:T(128)}, u32[]{:S(2)}) copy-start(u32[128]{0:T(128)} %constant.80) | copy-start | bytes 1540
  148.2 218.2 %copy-start.4 = (bf16[4,7168]{1,0:T(4,128)(2,1)S(1)}, bf16[4,7168]{1,0:T(4,128)(2,1)}, u32[]{:S(2)}) copy-start(bf16[4,7168]{1,0:T(4,128)(2,1)} %param.14) | copy-start | bytes 172036
  148.2 219.3 %copy-start.5 = (f32[7168]{0:T(1024)S(1)}, f32[7168]{0:T(1024)}, u32[]{:S(2)}) copy-start(f32[7168]{0:T(1024)} %param.20) | copy-start | bytes 86020
  161.0 205.5 %all-reduce.5.cloned.1.call-start = ((), (), s32[]{:S(2)}) async-start(), calls=%async_computation.3 | async-start | bytes 229376 | tf_op jit(solution)/shard_map/psum | solution.py:84
  398.0 97.8 %copy-start.6 = (f32[4,8]{1,0:T(4,128)S(1)}, f32[4,8]{1,0:T(4,128)}, u32[]{:S(2)}) copy-start(f32[4,8]{1,0:T(4,128)} %param.22) | copy-start | bytes 388
  492.2 18.8 %all-to-all-start.2 = ((bf16[16,1,3,7168]{3,2,1,0:T(4,128)(2,1)}), bf16[16,1,3,7168]{3,2,1,0:T(4,128)(2,1)S(1)}, u32[]{:S(2)}, u32[]{:S(2)}) async-start(bf16[16,1,3,7168]{3,2,1,0:T(4,128)(2,1)} %copy.27), calls=%async_computation.2 | async-start | bytes 1835008 | tf_op jit(solution)/shard_map/all_to_all | solution.py:126
Sparse Core Ops, SparseCore 0:
  19.8 109.7 all-gather.6
  161.1 120.0 all-reduce.6
  283.8 82.5 all-reduce.4
where the time goes:
time: 520 us; the launch traced here: 518 us
  waiting for transfers between devices  261 us (50%)
  blocking collectives  185 us (36%)
  matrix products  22.9 us (4%)
  other arithmetic  16.9 us (3%)
  local copies, waits for them, and re-layouts  15.1 us (3%)
  between operations  13.9 us (3%)
    unnamed x4, waiting for transfers between devices  119 us
    psum x1, blocking collectives, on_device(): expert_out = lax.psum(partial_out, 'dev').astype(jnp.bfloat16)  92.7 us
    psum x1, waiting for transfers between devices, on_device(): attention_out = lax.psum(node_part, 'dev')  83.4 us
    all_gather x2, blocking collectives, joined(): pieces = jax.tree.map(lambda part: lax.all_gather(part, axis), value)  61.7 us
    all_gather x1, waiting for transfers between devices, joined(): pieces = jax.tree.map(lambda part: lax.all_gather(part, axis), value)  44.7 us
    all_to_all x1, blocking collectives, on_device(): lax.all_to_all(outgoing, 'node', split_axis=0, concat_axis=0, tiled=True)  19.6 us
    all_to_all x1, waiting for transfers between devices, on_device(): lax.all_to_all(expert_out, 'node', split_axis=0, concat_axis=0, tiled=True)  14.6 us
    add x7, other arithmetic, join_partials(): left_sum * left_factor[..., None] + right_sum * right_factor[..., None]  10.7 us
  transfers between devices with their start and end apart: 4, of which 4 were waited for; matrix products, arithmetic and copies ran while one was open for 1% of the time, Pallas kernels for 0%

commit v1 on v0

v1 whole, which is shorter than its diff:
```python
import functools

import jax
import jax.numpy as jnp
from jax import lax
from jax.experimental import pallas as pl
from jax.experimental.pallas import tpu as pltpu
from jax.sharding import Mesh
from jax.sharding import PartitionSpec as P

PLANE = ("pair", "dev")
VMEM = pl.BlockSpec(memory_space=pltpu.VMEM)
SMEM = pl.BlockSpec(memory_space=pltpu.SMEM)
ANY = pl.BlockSpec(memory_space=pl.ANY)
NOTES = 128
LIMIT = 40 * 2**20
f32 = jnp.float32
bf16 = jnp.bfloat16


def exchange(blocks):
    return lax.all_to_all(blocks, PLANE, split_axis=0, concat_axis=0, tiled=True)


def other_core(value):
    return lax.ppermute(value, "core", [(0, 1), (1, 0)])


def thirds(value):
    high = value.astype(bf16).astype(f32)
    rest = value - high
    middle = rest.astype(bf16).astype(f32)
    return high, middle, rest - middle


def attend_kernel(
    lengths, routes, route_scores, query, cache, out, held, joined, arrivals
):
    rows, feature, positions = cache.shape
    heads = query.shape[2]
    tiles = joined.shape[0] - 1
    latent = tiles * NOTES
    dev = lax.axis_index("dev")
    dev_count = lax.axis_size("dev")
    copies = [
        pltpu.make_async_copy(cache.at[row], held.at[row], arrivals.at[row]) for row in range(rows)
    ]
    for copy in copies:
        copy.start()
    lane = lax.broadcasted_iota(jnp.int32, (heads, NOTES), 1)
    expert = lax.broadcasted_iota(jnp.int32, (heads, NOTES), 0) // dev_count
    position = lax.broadcasted_iota(jnp.int32, (heads, positions), 1)
    scale = feature**-0.5
    for row in range(rows):
        used = lengths[row] - dev * positions
        total_score = route_scores[row, 0]
        for k in range(1, routes.shape[1]):
            total_score = total_score + route_scores[row, k]
        named = jnp.zeros((heads, NOTES), f32)
        for k in range(routes.shape[1]):
            named = jnp.where(expert == routes[row, k], route_scores[row, k], named)
        coefficient = 2.5 * named / total_score
        copies[row].wait()
        scores = lax.dot_general(
            query[row], held[row], (((0,), (0,)), ((), ())), preferred_element_type=f32
        )
        scores = jnp.where(position < used, scores, -1e30)
        top = jnp.max(scores, axis=1, keepdims=True)
        weights = jnp.exp((scores - top) * scale)
        total = jnp.sum(weights, axis=1, keepdims=True)
        summed = lax.dot_general(
            weights.astype(bf16),
            held[row, :latent, :],
            (((1,), (1,)), ((), ())),
            preferred_element_type=f32,
        )
        mean = summed / total
        log_total = jnp.where(used > 0, top * scale + jnp.log(total), -1e30)
        notes = jnp.zeros((heads, NOTES), f32)
        for place, part in enumerate(thirds(log_total) + thirds(coefficient)):
            notes = jnp.where(lane == place, part, notes)
        for group in range(heads // 8):
            pair, core = group // 2, group % 2
            target = pl.ds(pair * 64 + core * rows + row, 8, stride=8)
            source = slice(group * 8, group * 8 + 8)
            for tile in range(tiles):
                joined[tile, target] = mean[source, tile * NOTES : (tile + 1) * NOTES]
            joined[tiles, target] = notes[source]
    for tile in range(tiles + 1):
        columns = slice(tile * NOTES, (tile + 1) * NOTES)
        out[:, :, columns] = joined[tile].astype(bf16).reshape(out.shape[0], out.shape[1], NOTES)


def attend(lengths, routes, route_scores, queries, cache, latent):
    rows, feature, positions = cache.shape
    heads = queries.shape[2]
    return pl.pallas_call(
        attend_kernel,
        out_shape=jax.ShapeDtypeStruct((heads // 2, 2 * rows, latent + NOTES), bf16),
        in_specs=[SMEM, SMEM, SMEM, VMEM, ANY],
        out_specs=VMEM,
        scratch_shapes=[
            pltpu.VMEM((rows, feature, positions), bf16),
            pltpu.VMEM((latent // NOTES + 1, heads * rows, NOTES), f32),
            pltpu.SemaphoreType.DMA((rows,)),
        ],
        compiler_params=pltpu.CompilerParams(vmem_limit_bytes=LIMIT),
        cost_estimate=pl.CostEstimate(
            flops=4 * rows * heads * feature * positions,
            bytes_accessed=2 * rows * feature * positions,
            transcendentals=rows * heads * positions,
        ),
        name="attend",
    )(lengths, routes, route_scores, queries, cache)


def project_kernel(arrived, up_own, up_other, out_own, out_other, part, coefficients):
    pairs, devs, rows, share = part.shape
    latent = up_own.shape[0]
    core = lax.axis_index("core")
    notes = arrived[:, :, latent:].astype(f32)
    lane = lax.broadcasted_iota(jnp.int32, notes.shape, 2)
    log_total = jnp.sum(jnp.where(lane < 3, notes, 0.0), axis=2, keepdims=True)
    coefficient = jnp.sum(
        jnp.where((lane >= 3) & (lane < 6), notes, 0.0), axis=2, keepdims=True
    )
    coefficient = coefficient.reshape(pairs, devs, 2 * rows, 1)[:, 0]
    coefficient = jnp.broadcast_to(coefficient, (pairs, 2 * rows, NOTES))
    coefficients[0] = coefficient[:, :rows]
    coefficients[1] = coefficient[:, rows:]
    log_total = log_total.reshape(pairs, devs, 2 * rows, 1)
    weight = jnp.exp(log_total - jnp.max(log_total, axis=1, keepdims=True))
    weight = weight / jnp.sum(weight, axis=1, keepdims=True)
    values = arrived[:, :, :latent].reshape(pairs, devs, 2 * rows, latent)
    attended = weight[:, 0] * values[:, 0].astype(f32)
    for dev in range(1, devs):
        attended = attended + weight[:, dev] * values[:, dev].astype(f32)
    attended = attended.reshape(pairs * 2 * rows, latent).astype(bf16)

    def head(up, is_own):
        value = jnp.dot(attended, up[...], preferred_element_type=f32)
        value = value.reshape(pairs, 2 * rows, -1)
        low, high = value[:, :rows], value[:, rows:]
        picked = jnp.where(core == (0 if is_own else 1), low, high)
        return picked.reshape(pairs * rows, -1).astype(bf16)

    own, other = head(up_own, True), head(up_other, False)
    for dev in range(devs):
        columns = slice(dev * share, (dev + 1) * share)
        value = jnp.dot(own, out_own[:, columns], preferred_element_type=f32)
        value = value + jnp.dot(other, out_other[:, columns], preferred_element_type=f32)
        part[:, dev] = value.astype(bf16).reshape(pairs, rows, share)


def project(arrived, up_own, up_other, out_own, out_other, pairs, devs):
    rows = arrived.shape[1] // 2
    width = out_own.shape[1]
    return pl.pallas_call(
        project_kernel,
        out_shape=(
            jax.ShapeDtypeStruct((pairs, devs, rows, width // devs), bf16),
            jax.ShapeDtypeStruct((2, pairs, rows, NOTES), f32),
        ),
        in_specs=[VMEM] * 5,
        out_specs=(VMEM, VMEM),
        compiler_params=pltpu.CompilerParams(vmem_limit_bytes=LIMIT),
        name="project",
    )(arrived, up_own, up_other, out_own, out_other)


def residual_kernel(arrived, hidden, residual, copies):
    share = residual.shape[1]
    start = pl.multiple_of(lax.axis_index("dev") * share, 128)
    total = hidden[:, pl.ds(start, share)].astype(f32)
    total = total + jnp.sum(arrived[...].astype(f32), axis=0)
    residual[...] = total
    copies[...] = jnp.broadcast_to(total.astype(bf16)[None], copies.shape)


def add_up(arrived, hidden):
    return pl.pallas_call(
        residual_kernel,
        out_shape=(
            jax.ShapeDtypeStruct(arrived.shape[1:], f32),
            jax.ShapeDtypeStruct(arrived.shape, bf16),
        ),
        in_specs=[VMEM, VMEM],
        out_specs=(VMEM, VMEM),
        compiler_params=pltpu.CompilerParams(vmem_limit_bytes=LIMIT),
        name="residual",
    )(arrived, hidden)


def experts_kernel(
    arrived,
    gain,
    coefficients,
    gate_own,
    gate_other,
    up_own,
    up_other,
    down_own,
    down_other,
    part,
    first,
    second,
    first_arrivals,
    second_arrivals,
):
    pairs, devs, rows, share = arrived.shape
    width = devs * share
    core = lax.axis_index("core")
    copies = []
    for dev in range(devs):
        band = pl.ds(dev * share, share)
        for place, source in enumerate((gate_own, gate_other, up_own, up_other)):
            copy = pltpu.make_async_copy(
                source.at[band], first.at[place, band], first_arrivals.at[place, dev]
            )
            copy.start()
            copies.append(copy)
    down_copies = []
    for place, source in enumerate((down_own, down_other)):
        copy = pltpu.make_async_copy(source, second.at[place], second_arrivals.at[place])
        copy.start()
        down_copies.append(copy)
    squares = jnp.zeros((pairs * rows, 1), f32)
    sums = [jnp.zeros((pairs * rows, first.shape[2]), f32) for _ in range(4)]
    for dev in range(devs):
        value = arrived[:, dev].astype(f32).reshape(pairs * rows, share)
        squares = squares + jnp.sum(value * value, axis=1, keepdims=True)
        value = (value * gain[dev : dev + 1, :]).astype(bf16)
        for place in range(4):
            copies[4 * dev + place].wait()
            sums[place] = sums[place] + jnp.dot(
                value, first[place, dev * share : (dev + 1) * share], preferred_element_type=f32
            )
    factor = lax.rsqrt(squares * (1.0 / width) + 1e-06)
    activated = []
    for place in range(2):
        gate, up = sums[place] * factor, sums[2 + place] * factor
        mix = jnp.where(core == place, coefficients[0], coefficients[1])
        mix = mix.reshape(pairs * rows, NOTES)[:, :1]
        activated.append((gate / (1.0 + jnp.exp(-gate)) * up * mix).astype(bf16))
    for copy in down_copies:
        copy.wait()
    for dev in range(devs):
        columns = slice(dev * share, (dev + 1) * share)
        value = jnp.dot(activated[0], second[0, :, columns], preferred_element_type=f32)
        value = value + jnp.dot(activated[1], second[1, :, columns], preferred_element_type=f32)
        part[:, dev] = value.astype(bf16).reshape(pairs, rows, share)


def experts(arrived, gain, coefficients, *weights):
    pairs, devs, rows, share = arrived.shape
    units = weights[0].shape[1]
    return pl.pallas_call(
        experts_kernel,
        out_shape=jax.ShapeDtypeStruct(arrived.shape, bf16),
        in_specs=[VMEM] * 3 + [ANY] * 6,
        out_specs=VMEM,
        scratch_shapes=[
            pltpu.VMEM((4, devs * share, units), bf16),
            pltpu.VMEM((2, units, devs * share), bf16),
            pltpu.SemaphoreType.DMA((4, devs)),
            pltpu.SemaphoreType.DMA((2,)),
        ],
        compiler_params=pltpu.CompilerParams(vmem_limit_bytes=LIMIT),
        name="experts",
    )(arrived, gain, coefficients, *weights)


def finish_kernel(arrived, residual, out):
    out[...] = residual[...] + jnp.sum(arrived[...].astype(f32), axis=0)


def finish(arrived, residual):
    return pl.pallas_call(
        finish_kernel,
        out_shape=jax.ShapeDtypeStruct(residual.shape, f32),
        in_specs=[VMEM, VMEM],
        out_specs=VMEM,
        compiler_params=pltpu.CompilerParams(vmem_limit_bytes=LIMIT),
        name="finish",
    )(arrived, residual)


def on_device(
    hidden,
    queries,
    latent_cache,
    lengths,
    value_up,
    output_weight,
    norm_gain,
    routes,
    route_scores,
    gate_weight,
    up_weight,
    down_weight,
):
    pairs, devs = lax.axis_size("pair"), lax.axis_size("dev")
    chips = pairs * devs
    rows, model_width = hidden.shape
    share = model_width // devs
    latent = value_up.shape[1]
    weights = [value_up[0], output_weight, gate_weight[0], up_weight[0], down_weight[0]]
    value_up, output_weight, gate_weight, up_weight, down_weight = weights
    value_other, output_other, gate_other, up_other, down_other = [other_core(w) for w in weights]

    parts = attend(
        lengths,
        routes,
        route_scores,
        jnp.swapaxes(queries, 1, 2),
        jnp.swapaxes(latent_cache, 1, 2),
        latent,
    )
    part, coefficients = project(
        exchange(parts), value_up, value_other, output_weight, output_other, pairs, devs
    )
    arrived = exchange(part.reshape(chips, rows, share))
    residual, copies = add_up(arrived, hidden)
    arrived = exchange(copies).reshape(pairs, devs, rows, share)
    part = experts(
        arrived,
        norm_gain.reshape(devs, share),
        coefficients,
        gate_weight,
        gate_other,
        up_weight,
        up_other,
        down_weight,
        down_other,
    )
    return finish(exchange(part.reshape(chips, rows, share)), residual)


def solution(mesh):
    nodes, devs = mesh.devices.shape
    planes = Mesh(mesh.devices.reshape(nodes // 2, 2, devs), ("pair", "core", "dev"))
    node = ("pair", "core")
    both = ("pair", "core", "dev")
    return jax.shard_map(
        on_device,
        mesh=planes,
        in_specs=(
            P(node, None),
            P(node, None, None),
            P(node, "dev", None),
            P(node),
            P(both, None, None),
            P(both, None),
            P(),
            P(node, None),
            P(node, None),
            P(node, None, "dev"),
            P(node, None, "dev"),
            P(node, "dev", None),
        ),
        out_specs=P(node, "dev"),
        check_vma=False,
    )
```

time: 520 us -> 112 us (0.22)
  waiting for transfers between devices: 261 us -> 25.4 us
  blocking collectives: 185 us -> 32.8 us
  Pallas kernels: 0 us -> 23.4 us
  matrix products: 22.9 us -> 0 us
  other arithmetic: 16.9 us -> 0 us
  starting transfers between devices: 3.72 us -> 18.3 us
  between operations: 13.9 us -> 0.11 us
    unnamed x4 -> x0, waiting for transfers between devices: 119 us -> none
    psum x1 -> x0, blocking collectives: 92.7 us -> none  [on_device(): expert_out = lax.psum(partial_out, 'dev').astype(jnp.bfloat16)]
    psum x1 -> x0, waiting for transfers between devices: 83.4 us -> none  [on_device(): attention_out = lax.psum(node_part, 'dev')]
    all_gather x2 -> x0, blocking collectives: 61.7 us -> none  [joined(): pieces = jax.tree.map(lambda part: lax.all_gather(part, axis), value)]
    all_gather x1 -> x0, waiting for transfers between devices: 44.7 us -> none  [joined(): pieces = jax.tree.map(lambda part: lax.all_gather(part, axis), value)]
    pallas_call x0 -> x5, Pallas kernels: none -> 23.4 us  [the longest x1 10.6 us: experts(): pl.pallas_call(experts_kernel, out_shape=jax.ShapeDtypeStruct(arrived.sha...]
    dot_general x9 -> x0, matrix products: 22.9 us -> none  [the longest x1 6.36 us: on_device(): jnp.einsum('secf,efd->secd', activated, down_weight, preferred_element_ty...]
    all_to_all x1 -> x2, starting transfers between devices: 3.63 us -> 17.2 us  [exchange(): lax.all_to_all(blocks, PLANE, split_axis=0, concat_axis=0, tiled=True)]
  transfers between devices with their start and end apart: 4 -> 7, of which waited for: 4 -> 3; matrix products, arithmetic and copies ran while one was open for 1% -> 0% of each run, Pallas kernels for 0% -> 11%
where the time goes in v1:
time: 112 us; the launch traced here: 111 us
  blocking collectives  32.8 us (29%)
  waiting for transfers between devices  25.4 us (23%)
  Pallas kernels  23.4 us (21%)
  starting transfers between devices  18.3 us (16%)
  local copies, waits for them, and re-layouts  10.9 us (10%)
    all_to_all x2, blocking collectives, exchange(): lax.all_to_all(blocks, PLANE, split_axis=0, concat_axis=0, tiled=True)  32.8 us
    all_to_all x2, waiting for transfers between devices, exchange(): lax.all_to_all(blocks, PLANE, split_axis=0, concat_axis=0, tiled=True)  24.1 us
    all_to_all x2, starting transfers between devices, exchange(): lax.all_to_all(blocks, PLANE, split_axis=0, concat_axis=0, tiled=True)  17.2 us
    unnamed x22, local copies, waits for them, and re-layouts  10.9 us
    pallas_call x1, Pallas kernels, experts(): pl.pallas_call(experts_kernel, out_shape=jax.ShapeDtypeStruct(arrived.sha...  10.6 us
    pallas_call x1, Pallas kernels, attend(): pl.pallas_call(attend_kernel, out_shape=jax.ShapeDtypeStruct((heads // 2,...  8.47 us
    pallas_call x1, Pallas kernels, project(): pl.pallas_call(project_kernel, out_shape=(jax.ShapeDtypeStruct((pairs, de...  2.54 us
  transfers between devices with their start and end apart: 7, of which 3 were waited for; matrix products, arithmetic and copies ran while one was open for 0% of the time, Pallas kernels for 11%

profile of v1, /device:TPU:0, one launch (start us, length us, event | category | flops | bytes accessed | tf_op | source)
XLA Modules:
  0.0 110.9 jit_solution(7774057959853940598)
XLA Ops:
  0.0 0.0 collective-permute-start.2
  0.0 0.5 collective-permute-start.3
  0.5 0.0 collective-permute-start.4
  0.5 0.5 collective-permute-start.1
  1.0 3.7 %copy-done = bf16[4,2048,576]{1,2,0:T(8,128)(2,1)S(1)} copy-done((bf16[4,2048,576]{1,2,0:T(8,128)(2,1)S(1)}, bf16[4,2048,576]{1,2,0:T(8,128)(2,1)}, u32[]{:S(2)}) %copy-start) | copy-done | bytes 9437208
  4.7 1.1 copy-done.4
  5.8 0.7 copy-done.7
  6.5 0.7 copy-done.8
  7.1 0.7 copy-done.9
  7.8 8.5 %attend.1 = bf16[64,8,640]{2,1,0:T(8,128)(2,1)} custom-call(s32[4]{0:T(128)S(1)} %copy-done.9, s32[4,8]{1,0:T(4,128)S(1)} %copy-done.7, f32[4,8]{1,0:T(4,128)S(1)} %copy-done.8, bf16[4,576,128]{2,1,0:T(8,128)(2,1)S(1)} %bitcast.16, bf16[4,576,2048]{2,1,0:T(8,128)(2,1)S(1)} %bitcast.9), custom_call_target="tpu_custom_call" | custom-call | flops 2415919104 | bytes 9437184 | tf_op jit(solution)/shard_map/attend/pallas_call | solution.py:97
  16.3 0.0 copy-start.6
  16.3 11.6 %all-to-all-start = ((bf16[64,8,640]{2,1,0:T(8,128)(2,1)}), bf16[64,8,640]{2,1,0:T(8,128)(2,1)S(1)}, u32[]{:S(2)}, u32[]{:S(2)}) async-start(bf16[64,8,640]{2,1,0:T(8,128)(2,1)} %attend.1), calls=%async_computation | async-start | bytes 1310720 | tf_op jit(solution)/shard_map/all_to_all | solution.py:22
  27.9 0.0 copy-start.10
  27.9 0.0 copy-done.5
  28.0 0.1 collective-permute-start
  28.0 1.3 %collective-permute-done.up_other = bf16[512,128]{1,0:T(8,128)(2,1)S(1)} collective-permute-done((bf16[512,128]{1,0:T(8,128)(2,1)S(1)}, bf16[512,128]{1,0:T(8,128)(2,1)S(1)}, u32[]{:S(2)}, u32[]{:S(2)}) %collective-permute-start) | collective-permute-done | bytes 131104 | tf_op jit(solution)/shard_map/ppermute | solution.py:26
  29.4 13.0 %all-to-all-done.arrived = bf16[64,8,640]{2,1,0:T(8,128)(2,1)S(1)} async-done(((bf16[64,8,640]{2,1,0:T(8,128)(2,1)}), bf16[64,8,640]{2,1,0:T(8,128)(2,1)S(1)}, u32[]{:S(2)}, u32[]{:S(2)}) %all-to-all-start) | async-done | bytes 655392 | tf_op jit(solution)/shard_map/all_to_all | solution.py:22
  42.4 0.0 collective-permute-done.1.out_other
  42.4 2.5 %project.1 = (bf16[8,8,4,896]{3,2,1,0:T(4,128)(2,1)S(1)}, f32[2,8,4,128]{3,2,1,0:T(4,128)S(1)}) custom-call(bf16[64,8,640]{2,1,0:T(8,128)(2,1)S(1)} %all-to-all-done.arrived, bf16[512,128]{1,0:T(8,128)(2,1)S(1)} %bitcast.19, bf16[512,128]{1,0:T(8,128)(2,1)S(1)} %collective-permute-done.up_other, bf16[128,7168]{1,0:T(8,128)(2,1)S(1)} %copy-done.3, ...), custom_call_target="tpu_custom_call" | custom-call | tf_op jit(solution)/shard_map/project/pallas_call | solution.py:158
  45.0 16.4 %all_to_all.20.arrived = bf16[64,4,896]{2,1,0:T(4,128)(2,1)S(1)} all-to-all(bf16[64,4,896]{2,1,0:T(4,128)(2,1)S(1)} %bitcast.17), channel_id=1, replica_groups=mesh['pair'=8,'core'=2,'dev'=8] {'pair','dev'}, dimensions={0} | all-to-all | bytes 917504 | tf_op jit(solution)/shard_map/all_to_all | solution.py:22
  61.4 1.0 residual.1
  62.4 5.5 %all-to-all-start.2 = ((bf16[64,4,896]{2,1,0:T(4,128)(2,1)}), bf16[64,4,896]{2,1,0:T(4,128)(2,1)S(1)}, u32[]{:S(2)}, u32[]{:S(2)}) async-start(bf16[64,4,896]{2,1,0:T(4,128)(2,1)} %get-tuple-element.10), calls=%async_computation.2 | async-start | bytes 917504 | tf_op jit(solution)/shard_map/all_to_all | solution.py:22
  68.0 11.0 %all-to-all-done.2 = bf16[64,4,896]{2,1,0:T(4,128)(2,1)S(1)} async-done(((bf16[64,4,896]{2,1,0:T(4,128)(2,1)}), bf16[64,4,896]{2,1,0:T(4,128)(2,1)S(1)}, u32[]{:S(2)}, u32[]{:S(2)}) %all-to-all-start.2) | async-done | bytes 458784 | tf_op jit(solution)/shard_map/all_to_all | solution.py:22
  79.0 0.0 collective-permute-done.2.gate_other
  79.0 0.0 collective-permute-done.3.up_other
  79.0 0.0 collective-permute-done.4.down_other
  79.0 0.0 copy-start.1
  79.0 2.0 %copy-done.1 = bf16[1,7168,256]{2,1,0:T(8,128)(2,1)S(1)} copy-done((bf16[1,7168,256]{2,1,0:T(8,128)(2,1)S(1)}, bf16[1,7168,256]{2,1,0:T(8,128)(2,1)}, u32[]{:S(2)}) %copy-start.1) | copy-done | bytes 3670040
  81.1 2.0 %copy-done.2 = bf16[1,7168,256]{2,1,0:T(8,128)(2,1)S(1)} copy-done((bf16[1,7168,256]{2,1,0:T(8,128)(2,1)S(1)}, bf16[1,7168,256]{2,1,0:T(8,128)(2,1)}, u32[]{:S(2)}) %copy-start.2) | copy-done | bytes 3670040
  83.1 10.6 %experts.1 = bf16[8,8,4,896]{3,2,1,0:T(4,128)(2,1)S(1)} custom-call(bf16[8,8,4,896]{3,2,1,0:T(4,128)(2,1)S(1)} %bitcast.14, f32[8,896]{1,0:T(8,128)S(1)} %reshape.14.gain, f32[2,8,4,128]{3,2,1,0:T(4,128)S(1)} %get-tuple-element.11.coefficients, bf16[7168,256]{1,0:T(8,128)(2,1)S(1)} %bitcast.11, bf16[7168,256]{1,0:T(8,128)(2,1)} %collective-permute-done.2.gate_other, ...), custom_call_target="tpu_custom_call" | custom-call | tf_op jit(solution)/shard_map/experts/pallas_call | solution.py:257
  93.7 16.4 %all_to_all.21.arrived = bf16[64,4,896]{2,1,0:T(4,128)(2,1)S(1)} all-to-all(bf16[64,4,896]{2,1,0:T(4,128)(2,1)S(1)} %bitcast.15), channel_id=1, replica_groups=mesh['pair'=8,'core'=2,'dev'=8] {'pair','dev'}, dimensions={0} | all-to-all | bytes 917504 | tf_op jit(solution)/shard_map/all_to_all | solution.py:22
  110.1 0.8 finish.1
  (12 shorter events, 0.0 us)
Async XLA Ops:
  0.0 79.0 %collective-permute-start.2 = (bf16[7168,256]{1,0:T(8,128)(2,1)}, bf16[7168,256]{1,0:T(8,128)(2,1)}, u32[]{:S(2)}, u32[]{:S(2)}) collective-permute-start(bf16[7168,256]{1,0:T(8,128)(2,1)} %bitcast.10), channel_id=1, source_target_pairs={{0,8},{8,0},{1,9},{9,1},{2,10},{10,2},{3,11},{11,3},{4,12},{12,4},... | collective-permute-start | bytes 11010056 | tf_op jit(solution)/shard_map/ppermute | solution.py:26
  0.0 79.0 %collective-permute-start.3 = (bf16[7168,256]{1,0:T(8,128)(2,1)}, bf16[7168,256]{1,0:T(8,128)(2,1)}, u32[]{:S(2)}, u32[]{:S(2)}) collective-permute-start(bf16[7168,256]{1,0:T(8,128)(2,1)} %bitcast.12), channel_id=1, source_target_pairs={{0,8},{8,0},{1,9},{9,1},{2,10},{10,2},{3,11},{11,3},{4,12},{12,4},... | collective-permute-start | bytes 11010056 | tf_op jit(solution)/shard_map/ppermute | solution.py:26
  0.5 78.5 %collective-permute-start.4 = (bf16[256,7168]{1,0:T(8,128)(2,1)}, bf16[256,7168]{1,0:T(8,128)(2,1)}, u32[]{:S(2)}, u32[]{:S(2)}) collective-permute-start(bf16[256,7168]{1,0:T(8,128)(2,1)} %bitcast.20), channel_id=1, source_target_pairs={{0,8},{8,0},{1,9},{9,1},{2,10},{10,2},{3,11},{11,3},{4,12},{12,4},... | collective-permute-start | bytes 11010056 | tf_op jit(solution)/shard_map/ppermute | solution.py:26
  0.5 41.9 %collective-permute-start.1 = (bf16[128,7168]{1,0:T(8,128)(2,1)}, bf16[128,7168]{1,0:T(8,128)(2,1)}, u32[]{:S(2)}, u32[]{:S(2)}) collective-permute-start(bf16[128,7168]{1,0:T(8,128)(2,1)} %out_own.1), channel_id=1, source_target_pairs={{0,8},{8,0},{1,9},{9,1},{2,10},{10,2},{3,11},{11,3},{4,12},{12,4},... | collective-permute-start | bytes 5505032 | tf_op jit(solution)/shard_map/ppermute | solution.py:26
  1.0 3.7 %copy-start = (bf16[4,2048,576]{1,2,0:T(8,128)(2,1)S(1)}, bf16[4,2048,576]{1,2,0:T(8,128)(2,1)}, u32[]{:S(2)}) copy-start(bf16[4,2048,576]{1,2,0:T(8,128)(2,1)} %param.14) | copy-start | bytes 28311556
  4.7 1.1 copy-start.4
  5.8 0.7 copy-start.7
  6.5 0.7 copy-start.8
  7.1 0.7 copy-start.9
  7.8 20.2 %copy-start.5 = (bf16[1,512,128]{2,1,0:T(8,128)(2,1)S(1)}, bf16[1,512,128]{2,1,0:T(8,128)(2,1)}, u32[]{:S(2)}) copy-start(bf16[1,512,128]{2,1,0:T(8,128)(2,1)} %param.16) | copy-start | bytes 393220
  7.8 34.6 %copy-start.3 = (bf16[128,7168]{1,0:T(8,128)(2,1)S(1)}, bf16[128,7168]{1,0:T(8,128)(2,1)}, u32[]{:S(2)}) copy-start(bf16[128,7168]{1,0:T(8,128)(2,1)} %out_own.1) | copy-start | bytes 5505028
  16.3 45.1 %copy-start.6 = (bf16[4,7168]{1,0:T(4,128)(2,1)S(1)}, bf16[4,7168]{1,0:T(4,128)(2,1)}, u32[]{:S(2)}) copy-start(bf16[4,7168]{1,0:T(4,128)(2,1)} %hidden.1) | copy-start | bytes 172036
  16.3 26.1 %all-to-all-start = ((bf16[64,8,640]{2,1,0:T(8,128)(2,1)}), bf16[64,8,640]{2,1,0:T(8,128)(2,1)S(1)}, u32[]{:S(2)}, u32[]{:S(2)}) async-start(bf16[64,8,640]{2,1,0:T(8,128)(2,1)} %attend.1), calls=%async_computation | async-start | bytes 1310720 | tf_op jit(solution)/shard_map/all_to_all | solution.py:22
  27.9 40.0 %copy-start.10 = (f32[7168]{0:T(1024)S(1)}, f32[7168]{0:T(1024)}, u32[]{:S(2)}) copy-start(f32[7168]{0:T(1024)} %param.18) | copy-start | bytes 86020
  28.0 1.4 %collective-permute-start = (bf16[512,128]{1,0:T(8,128)(2,1)S(1)}, bf16[512,128]{1,0:T(8,128)(2,1)S(1)}, u32[]{:S(2)}, u32[]{:S(2)}) collective-permute-start(bf16[512,128]{1,0:T(8,128)(2,1)S(1)} %bitcast.18), channel_id=1, source_target_pairs={{0,8},{8,0},{1,9},{9,1},{2,10},{10,2},{3,11},{11,3},{4,12},{12,4},... | collective-permute-start | bytes 393224 | tf_op jit(solution)/shard_map/ppermute | solution.py:26
  62.4 16.6 %all-to-all-start.2 = ((bf16[64,4,896]{2,1,0:T(4,128)(2,1)}), bf16[64,4,896]{2,1,0:T(4,128)(2,1)S(1)}, u32[]{:S(2)}, u32[]{:S(2)}) async-start(bf16[64,4,896]{2,1,0:T(4,128)(2,1)} %get-tuple-element.10), calls=%async_computation.2 | async-start | bytes 917504 | tf_op jit(solution)/shard_map/all_to_all | solution.py:22
  79.0 2.0 %copy-start.1 = (bf16[1,7168,256]{2,1,0:T(8,128)(2,1)S(1)}, bf16[1,7168,256]{2,1,0:T(8,128)(2,1)}, u32[]{:S(2)}) copy-start(bf16[1,7168,256]{2,1,0:T(8,128)(2,1)} %param.21) | copy-start | bytes 11010052
  81.1 2.0 %copy-start.2 = (bf16[1,7168,256]{2,1,0:T(8,128)(2,1)S(1)}, bf16[1,7168,256]{2,1,0:T(8,128)(2,1)}, u32[]{:S(2)}) copy-start(bf16[1,7168,256]{2,1,0:T(8,128)(2,1)} %param.22) | copy-start | bytes 11010052

commit v2 on v1

--- a/solution.py
+++ b/solution.py
@@ -1,5 +1,3 @@
-import functools
-
 import jax
 import jax.numpy as jnp
 from jax import lax
@@ -13,6 +11,8 @@
 SMEM = pl.BlockSpec(memory_space=pltpu.SMEM)
 ANY = pl.BlockSpec(memory_space=pl.ANY)
 NOTES = 128
+SLABS = 8
+PIECES = 1
 LIMIT = 40 * 2**20
 f32 = jnp.float32
 bf16 = jnp.bfloat16
@@ -34,7 +34,20 @@
 
 
 def attend_kernel(
-    lengths, routes, route_scores, query, cache, out, held, joined, arrivals
+    lengths_in,
+    routes_in,
+    scores_in,
+    query_in,
+    cache,
+    out,
+    held,
+    joined,
+    query,
+    lengths,
+    routes,
+    route_scores,
+    arrivals,
+    small_arrivals,
 ):
     rows, feature, positions = cache.shape
     heads = query.shape[2]
@@ -42,28 +55,58 @@
     latent = tiles * NOTES
     dev = lax.axis_index("dev")
     dev_count = lax.axis_size("dev")
+    small = [
+        pltpu.make_async_copy(source, target, small_arrivals.at[place])
+        for place, (source, target) in enumerate(
+            (
+                (query_in, query),
+                (lengths_in, lengths),
+                (routes_in, routes),
+                (scores_in, route_scores),
+            )
+        )
+    ]
     copies = [
-        pltpu.make_async_copy(cache.at[row], held.at[row], arrivals.at[row]) for row in range(rows)
+        [
+            pltpu.make_async_copy(
+                cache.at[row, pl.ds(start, feature // PIECES)],
+                held.at[row, pl.ds(start, feature // PIECES)],
+                arrivals.at[row],
+            )
+            for start in range(0, feature, feature // PIECES)
+        ]
+        for row in range(rows)
     ]
-    for copy in copies:
+    for copy in small + sum(copies, []):
         copy.start()
+    for copy in small:
+        copy.wait()
     lane = lax.broadcasted_iota(jnp.int32, (heads, NOTES), 1)
     expert = lax.broadcasted_iota(jnp.int32, (heads, NOTES), 0) // dev_count
     position = lax.broadcasted_iota(jnp.int32, (heads, positions), 1)
     scale = feature**-0.5
+    mixes = []
     for row in range(rows):
-        used = lengths[row] - dev * positions
         total_score = route_scores[row, 0]
         for k in range(1, routes.shape[1]):
             total_score = total_score + route_scores[row, k]
         named = jnp.zeros((heads, NOTES), f32)
         for k in range(routes.shape[1]):
             named = jnp.where(expert == routes[row, k], route_scores[row, k], named)
-        coefficient = 2.5 * named / total_score
-        copies[row].wait()
-        scores = lax.dot_general(
+        mixes.append(2.5 * named / total_score)
+
+    def raw_scores(row):
+        pltpu.make_async_copy(cache.at[row], held.at[row], arrivals.at[row]).wait()
+        return lax.dot_general(
             query[row], held[row], (((0,), (0,)), ((), ())), preferred_element_type=f32
         )
+
+    following = raw_scores(0)
+    for row in range(rows):
+        scores = following
+        if row + 1 < rows:
+            following = raw_scores(row + 1)
+        used = lengths[row] - dev * positions
         scores = jnp.where(position < used, scores, -1e30)
         top = jnp.max(scores, axis=1, keepdims=True)
         weights = jnp.exp((scores - top) * scale)
@@ -77,7 +120,7 @@
         mean = summed / total
         log_total = jnp.where(used > 0, top * scale + jnp.log(total), -1e30)
         notes = jnp.zeros((heads, NOTES), f32)
-        for place, part in enumerate(thirds(log_total) + thirds(coefficient)):
+        for place, part in enumerate(thirds(log_total) + thirds(mixes[row])):
             notes = jnp.where(lane == place, part, notes)
         for group in range(heads // 8):
             pair, core = group // 2, group % 2
@@ -91,18 +134,27 @@
         out[:, :, columns] = joined[tile].astype(bf16).reshape(out.shape[0], out.shape[1], NOTES)
 
 
+def pinned(value, space=pltpu.HBM):
+    return pltpu.with_memory_space_constraint(value, space)
+
+
 def attend(lengths, routes, route_scores, queries, cache, latent):
     rows, feature, positions = cache.shape
     heads = queries.shape[2]
     return pl.pallas_call(
         attend_kernel,
         out_shape=jax.ShapeDtypeStruct((heads // 2, 2 * rows, latent + NOTES), bf16),
-        in_specs=[SMEM, SMEM, SMEM, VMEM, ANY],
+        in_specs=[ANY] * 5,
         out_specs=VMEM,
         scratch_shapes=[
             pltpu.VMEM((rows, feature, positions), bf16),
             pltpu.VMEM((latent // NOTES + 1, heads * rows, NOTES), f32),
+            pltpu.VMEM(queries.shape, bf16),
+            pltpu.SMEM(lengths.shape, jnp.int32),
+            pltpu.SMEM(routes.shape, jnp.int32),
+            pltpu.SMEM(route_scores.shape, f32),
             pltpu.SemaphoreType.DMA((rows,)),
+            pltpu.SemaphoreType.DMA((4,)),
         ],
         compiler_params=pltpu.CompilerParams(vmem_limit_bytes=LIMIT),
         cost_estimate=pl.CostEstimate(
@@ -111,10 +163,19 @@
             transcendentals=rows * heads * positions,
         ),
         name="attend",
-    )(lengths, routes, route_scores, queries, cache)
-
-
-def project_kernel(arrived, up_own, up_other, out_own, out_other, part, coefficients):
+    )(*[pinned(value) for value in (lengths, routes, route_scores, queries, cache)])
+
+
+def project_kernel(
+    arrived, up_own, up_other, out_own, other_in, part, coefficients, out_other, arrivals
+):
+    copies = []
+    for cut in range(SLABS):
+        band = pl.ds(cut * (out_other.shape[0] // SLABS), out_other.shape[0] // SLABS)
+        copies.append(
+            pltpu.make_async_copy(other_in.at[band], out_other.at[band], arrivals.at[cut])
+        )
+        copies[-1].start()
     pairs, devs, rows, share = part.shape
     latent = up_own.shape[0]
     core = lax.axis_index("core")
@@ -145,6 +206,8 @@
         return picked.reshape(pairs * rows, -1).astype(bf16)
 
     own, other = head(up_own, True), head(up_other, False)
+    for copy in copies:
+        copy.wait()
     for dev in range(devs):
         columns = slice(dev * share, (dev + 1) * share)
         value = jnp.dot(own, out_own[:, columns], preferred_element_type=f32)
@@ -161,11 +224,15 @@
             jax.ShapeDtypeStruct((pairs, devs, rows, width // devs), bf16),
             jax.ShapeDtypeStruct((2, pairs, rows, NOTES), f32),
         ),
-        in_specs=[VMEM] * 5,
+        in_specs=[VMEM] * 4 + [ANY],
         out_specs=(VMEM, VMEM),
+        scratch_shapes=[
+            pltpu.VMEM(out_other.shape, bf16),
+            pltpu.SemaphoreType.DMA((SLABS,)),
+        ],
         compiler_params=pltpu.CompilerParams(vmem_limit_bytes=LIMIT),
         name="project",
-    )(arrived, up_own, up_other, out_own, out_other)
+    )(arrived, up_own, up_other, out_own, pinned(out_other))
 
 
 def residual_kernel(arrived, hidden, residual, copies):
@@ -209,29 +276,36 @@
 ):
     pairs, devs, rows, share = arrived.shape
     width = devs * share
+    units = first.shape[2]
     core = lax.axis_index("core")
-    copies = []
+    first_copies, second_copies = [], []
     for dev in range(devs):
         band = pl.ds(dev * share, share)
         for place, source in enumerate((gate_own, gate_other, up_own, up_other)):
-            copy = pltpu.make_async_copy(
-                source.at[band], first.at[place, band], first_arrivals.at[place, dev]
+            first_copies.append(
+                pltpu.make_async_copy(
+                    source.at[band], first.at[place, band], first_arrivals.at[place, dev]
+                )
             )
-            copy.start()
-            copies.append(copy)
-    down_copies = []
     for place, source in enumerate((down_own, down_other)):
-        copy = pltpu.make_async_copy(source, second.at[place], second_arrivals.at[place])
+        for cut in range(SLABS):
+            band = pl.ds(cut * (units // SLABS), units // SLABS)
+            second_copies.append(
+                pltpu.make_async_copy(
+                    source.at[band], second.at[place, band], second_arrivals.at[place, cut]
+                )
+            )
+    for copy in first_copies + second_copies:
         copy.start()
-        down_copies.append(copy)
     squares = jnp.zeros((pairs * rows, 1), f32)
-    sums = [jnp.zeros((pairs * rows, first.shape[2]), f32) for _ in range(4)]
+    sums = [jnp.zeros((pairs * rows, units), f32) for _ in range(4)]
     for dev in range(devs):
         value = arrived[:, dev].astype(f32).reshape(pairs * rows, share)
         squares = squares + jnp.sum(value * value, axis=1, keepdims=True)
         value = (value * gain[dev : dev + 1, :]).astype(bf16)
         for place in range(4):
-            copies[4 * dev + place].wait()
+            first_copies[4 * dev + place].wait()
+        for place in range(4):
             sums[place] = sums[place] + jnp.dot(
                 value, first[place, dev * share : (dev + 1) * share], preferred_element_type=f32
             )
@@ -242,7 +316,7 @@
         mix = jnp.where(core == place, coefficients[0], coefficients[1])
         mix = mix.reshape(pairs * rows, NOTES)[:, :1]
         activated.append((gate / (1.0 + jnp.exp(-gate)) * up * mix).astype(bf16))
-    for copy in down_copies:
+    for copy in second_copies:
         copy.wait()
     for dev in range(devs):
         columns = slice(dev * share, (dev + 1) * share)
@@ -263,11 +337,11 @@
             pltpu.VMEM((4, devs * share, units), bf16),
             pltpu.VMEM((2, units, devs * share), bf16),
             pltpu.SemaphoreType.DMA((4, devs)),
-            pltpu.SemaphoreType.DMA((2,)),
+            pltpu.SemaphoreType.DMA((2, SLABS)),
         ],
         compiler_params=pltpu.CompilerParams(vmem_limit_bytes=LIMIT),
         name="experts",
-    )(arrived, gain, coefficients, *weights)
+    )(arrived, gain, coefficients, *[pinned(weight) for weight in weights])
 
 
 def finish_kernel(arrived, residual, out):
@@ -304,10 +378,16 @@
     rows, model_width = hidden.shape
     share = model_width // devs
     latent = value_up.shape[1]
-    weights = [value_up[0], output_weight, gate_weight[0], up_weight[0], down_weight[0]]
-    value_up, output_weight, gate_weight, up_weight, down_weight = weights
-    value_other, output_other, gate_other, up_other, down_other = [other_core(w) for w in weights]
-
+    value_up, gate_weight, up_weight, down_weight = (
+        value_up[0],
+        gate_weight[0],
+        up_weight[0],
+        down_weight[0],
+    )
+    value_other, output_other, gate_other, up_other, down_other = [
+        other_core(weight)
+        for weight in (value_up, output_weight, gate_weight, up_weight, down_weight)
+    ]
     parts = attend(
         lengths,
         routes,

time: 112 us -> 99.3 us (0.89)
  local copies, waits for them, and re-layouts: 10.9 us -> 0.03 us
  Pallas kernels: 23.4 us -> 22.2 us
    unnamed x22 -> x8, local copies, waits for them, and re-layouts: 10.9 us -> 0.02 us
    pallas_call x1, Pallas kernels: 10.6 us -> 9.21 us  [experts(): pl.pallas_call(experts_kernel, out_shape=jax.ShapeDtypeStruct(arrived.sha...]
  transfers between devices with their start and end apart: 7 -> 7, of which waited for: 3 -> 3; matrix products, arithmetic and copies ran while one was open for 0% -> 0% of each run, Pallas kernels for 11% -> 12%
where the time goes in v2:
time: 99.3 us; the launch traced here: 98.9 us
  blocking collectives  32.8 us (33%)
  waiting for transfers between devices  25.4 us (26%)
  Pallas kernels  22.2 us (22%)
  starting transfers between devices  18.3 us (18%)
    all_to_all x2, blocking collectives, exchange(): lax.all_to_all(blocks, PLANE, split_axis=0, concat_axis=0, tiled=True)  32.8 us
    all_to_all x2, waiting for transfers between devices, exchange(): lax.all_to_all(blocks, PLANE, split_axis=0, concat_axis=0, tiled=True)  24.1 us
    all_to_all x2, starting transfers between devices, exchange(): lax.all_to_all(blocks, PLANE, split_axis=0, concat_axis=0, tiled=True)  17.2 us
    pallas_call x1, Pallas kernels, experts(): pl.pallas_call(experts_kernel, out_shape=jax.ShapeDtypeStruct(arrived.sha...  9.21 us
    pallas_call x1, Pallas kernels, attend(): pl.pallas_call(attend_kernel, out_shape=jax.ShapeDtypeStruct((heads // 2,...  8.85 us
    pallas_call x1, Pallas kernels, project(): pl.pallas_call(project_kernel, out_shape=(jax.ShapeDtypeStruct((pairs, de...  2.37 us
  transfers between devices with their start and end apart: 7, of which 3 were waited for; matrix products, arithmetic and copies ran while one was open for 0% of the time, Pallas kernels for 12%

profile of v2, /device:TPU:0, one launch (start us, length us, event | category | flops | bytes accessed | tf_op | source)
XLA Modules:
  0.0 98.9 jit_solution(9933419709036047861)
XLA Ops:
  0.0 0.0 collective-permute-start.2
  0.0 0.5 collective-permute-start.3
  0.5 0.0 collective-permute-start.4
  0.5 0.5 collective-permute-start.1
  1.0 0.0 copy-start.1
  1.0 0.0 copy-start
  1.0 8.8 %attend.1 = bf16[64,8,640]{2,1,0:T(8,128)(2,1)} custom-call(s32[4]{0:T(128)} %lengths_in.1, s32[4,8]{1,0:T(4,128)} %routes_in.1, f32[4,8]{1,0:T(4,128)} %scores_in.1, bf16[4,576,128]{2,1,0:T(8,128)(2,1)} %bitcast.21, bf16[4,576,2048]{2,1,0:T(8,128)(2,1)} %bitcast.14), custom_call_target="tpu_custom_call" | custom-call | flops 2415919104 | bytes 9437184 | tf_op jit(solution)/shard_map/attend/pallas_call | solution.py:144
  9.9 0.0 copy-start.2
  9.9 11.6 %all-to-all-start = ((bf16[64,8,640]{2,1,0:T(8,128)(2,1)}), bf16[64,8,640]{2,1,0:T(8,128)(2,1)S(1)}, u32[]{:S(2)}, u32[]{:S(2)}) async-start(bf16[64,8,640]{2,1,0:T(8,128)(2,1)} %attend.1), calls=%async_computation | async-start | bytes 1310720 | tf_op jit(solution)/shard_map/all_to_all | solution.py:22
  21.5 0.0 copy-start.3
  21.6 0.0 copy-done.1
  21.6 0.1 collective-permute-start
  21.7 1.3 %collective-permute-done.up_other = bf16[512,128]{1,0:T(8,128)(2,1)S(1)} collective-permute-done((bf16[512,128]{1,0:T(8,128)(2,1)S(1)}, bf16[512,128]{1,0:T(8,128)(2,1)S(1)}, u32[]{:S(2)}, u32[]{:S(2)}) %collective-permute-start) | collective-permute-done | bytes 131104 | tf_op jit(solution)/shard_map/ppermute | solution.py:26
  23.0 13.0 %all-to-all-done.arrived = bf16[64,8,640]{2,1,0:T(8,128)(2,1)S(1)} async-done(((bf16[64,8,640]{2,1,0:T(8,128)(2,1)}), bf16[64,8,640]{2,1,0:T(8,128)(2,1)S(1)}, u32[]{:S(2)}, u32[]{:S(2)}) %all-to-all-start) | async-done | bytes 655392 | tf_op jit(solution)/shard_map/all_to_all | solution.py:22
  36.0 0.0 collective-permute-done.1.other_in
  36.0 0.0 copy-done
  36.0 2.4 %project.1 = (bf16[8,8,4,896]{3,2,1,0:T(4,128)(2,1)S(1)}, f32[2,8,4,128]{3,2,1,0:T(4,128)S(1)}) custom-call(bf16[64,8,640]{2,1,0:T(8,128)(2,1)S(1)} %all-to-all-done.arrived, bf16[512,128]{1,0:T(8,128)(2,1)S(1)} %bitcast.13, bf16[512,128]{1,0:T(8,128)(2,1)S(1)} %collective-permute-done.up_other, bf16[128,7168]{1,0:T(8,128)(2,1)S(1)} %copy-done, ...), custom_call_target="tpu_custom_call" | custom-call | tf_op jit(solution)/shard_map/project/pallas_call | solution.py:221
  38.4 16.4 %all_to_all.20.arrived = bf16[64,4,896]{2,1,0:T(4,128)(2,1)S(1)} all-to-all(bf16[64,4,896]{2,1,0:T(4,128)(2,1)S(1)} %bitcast.11), channel_id=1, replica_groups=mesh['pair'=8,'core'=2,'dev'=8] {'pair','dev'}, dimensions={0} | all-to-all | bytes 917504 | tf_op jit(solution)/shard_map/all_to_all | solution.py:22
  54.8 0.0 copy-done.2
  54.8 1.0 %residual.1 = (f32[4,896]{1,0:T(4,128)S(1)}, bf16[64,4,896]{2,1,0:T(4,128)(2,1)}) custom-call(bf16[64,4,896]{2,1,0:T(4,128)(2,1)S(1)} %all_to_all.20.arrived, bf16[4,7168]{1,0:T(4,128)(2,1)S(1)} %copy-done.2), custom_call_target="tpu_custom_call" | custom-call | tf_op jit(solution)/shard_map/residual/pallas_call | solution.py:248
  55.9 5.5 %all-to-all-start.2 = ((bf16[64,4,896]{2,1,0:T(4,128)(2,1)}), bf16[64,4,896]{2,1,0:T(4,128)(2,1)S(1)}, u32[]{:S(2)}, u32[]{:S(2)}) async-start(bf16[64,4,896]{2,1,0:T(4,128)(2,1)} %get-tuple-element.10), calls=%async_computation.2 | async-start | bytes 917504 | tf_op jit(solution)/shard_map/all_to_all | solution.py:22
  61.4 0.0 copy-done.3
  61.4 11.0 %all-to-all-done.2 = bf16[64,4,896]{2,1,0:T(4,128)(2,1)S(1)} async-done(((bf16[64,4,896]{2,1,0:T(4,128)(2,1)}), bf16[64,4,896]{2,1,0:T(4,128)(2,1)S(1)}, u32[]{:S(2)}, u32[]{:S(2)}) %all-to-all-start.2) | async-done | bytes 458784 | tf_op jit(solution)/shard_map/all_to_all | solution.py:22
  72.5 0.0 collective-permute-done.2.gate_other
  72.5 0.0 collective-permute-done.3.up_other
  72.5 0.0 collective-permute-done.4.down_other
  72.5 9.2 %experts.1 = bf16[8,8,4,896]{3,2,1,0:T(4,128)(2,1)S(1)} custom-call(bf16[8,8,4,896]{3,2,1,0:T(4,128)(2,1)S(1)} %bitcast.9, f32[8,896]{1,0:T(8,128)S(1)} %reshape.14.gain, f32[2,8,4,128]{3,2,1,0:T(4,128)S(1)} %get-tuple-element.11.coefficients, bf16[7168,256]{1,0:T(8,128)(2,1)} %bitcast.16, bf16[7168,256]{1,0:T(8,128)(2,1)} %collective-permute-done.2.gate_other, ...), custom_call_target="tpu_custom_call" | custom-call | tf_op jit(solution)/shard_map/experts/pallas_call | solution.py:331
  81.7 16.4 %all_to_all.21.arrived = bf16[64,4,896]{2,1,0:T(4,128)(2,1)S(1)} all-to-all(bf16[64,4,896]{2,1,0:T(4,128)(2,1)S(1)} %bitcast.10), channel_id=1, replica_groups=mesh['pair'=8,'core'=2,'dev'=8] {'pair','dev'}, dimensions={0} | all-to-all | bytes 917504 | tf_op jit(solution)/shard_map/all_to_all | solution.py:22
  98.1 0.8 finish.1
  (1 shorter events, 0.0 us)
Async XLA Ops:
  0.0 72.5 %collective-permute-start.2 = (bf16[7168,256]{1,0:T(8,128)(2,1)}, bf16[7168,256]{1,0:T(8,128)(2,1)}, u32[]{:S(2)}, u32[]{:S(2)}) collective-permute-start(bf16[7168,256]{1,0:T(8,128)(2,1)} %bitcast.15), channel_id=1, source_target_pairs={{0,8},{8,0},{1,9},{9,1},{2,10},{10,2},{3,11},{11,3},{4,12},{12,4},... | collective-permute-start | bytes 11010056 | tf_op jit(solution)/shard_map/ppermute | solution.py:26
  0.0 72.5 %collective-permute-start.3 = (bf16[7168,256]{1,0:T(8,128)(2,1)}, bf16[7168,256]{1,0:T(8,128)(2,1)}, u32[]{:S(2)}, u32[]{:S(2)}) collective-permute-start(bf16[7168,256]{1,0:T(8,128)(2,1)} %bitcast.17), channel_id=1, source_target_pairs={{0,8},{8,0},{1,9},{9,1},{2,10},{10,2},{3,11},{11,3},{4,12},{12,4},... | collective-permute-start | bytes 11010056 | tf_op jit(solution)/shard_map/ppermute | solution.py:26
  0.5 72.0 %collective-permute-start.4 = (bf16[256,7168]{1,0:T(8,128)(2,1)}, bf16[256,7168]{1,0:T(8,128)(2,1)}, u32[]{:S(2)}, u32[]{:S(2)}) collective-permute-start(bf16[256,7168]{1,0:T(8,128)(2,1)} %bitcast.19), channel_id=1, source_target_pairs={{0,8},{8,0},{1,9},{9,1},{2,10},{10,2},{3,11},{11,3},{4,12},{12,4},... | collective-permute-start | bytes 11010056 | tf_op jit(solution)/shard_map/ppermute | solution.py:26
  0.5 35.5 %collective-permute-start.1 = (bf16[128,7168]{1,0:T(8,128)(2,1)}, bf16[128,7168]{1,0:T(8,128)(2,1)}, u32[]{:S(2)}, u32[]{:S(2)}) collective-permute-start(bf16[128,7168]{1,0:T(8,128)(2,1)} %out_own.1), channel_id=1, source_target_pairs={{0,8},{8,0},{1,9},{9,1},{2,10},{10,2},{3,11},{11,3},{4,12},{12,4},... | collective-permute-start | bytes 5505032 | tf_op jit(solution)/shard_map/ppermute | solution.py:26
  1.0 20.5 %copy-start.1 = (bf16[1,512,128]{2,1,0:T(8,128)(2,1)S(1)}, bf16[1,512,128]{2,1,0:T(8,128)(2,1)}, u32[]{:S(2)}) copy-start(bf16[1,512,128]{2,1,0:T(8,128)(2,1)} %param.16) | copy-start | bytes 393220
  1.0 35.0 %copy-start = (bf16[128,7168]{1,0:T(8,128)(2,1)S(1)}, bf16[128,7168]{1,0:T(8,128)(2,1)}, u32[]{:S(2)}) copy-start(bf16[128,7168]{1,0:T(8,128)(2,1)} %out_own.1) | copy-start | bytes 5505028
  9.9 45.0 %copy-start.2 = (bf16[4,7168]{1,0:T(4,128)(2,1)S(1)}, bf16[4,7168]{1,0:T(4,128)(2,1)}, u32[]{:S(2)}) copy-start(bf16[4,7168]{1,0:T(4,128)(2,1)} %hidden.1) | copy-start | bytes 172036
  9.9 26.1 %all-to-all-start = ((bf16[64,8,640]{2,1,0:T(8,128)(2,1)}), bf16[64,8,640]{2,1,0:T(8,128)(2,1)S(1)}, u32[]{:S(2)}, u32[]{:S(2)}) async-start(bf16[64,8,640]{2,1,0:T(8,128)(2,1)} %attend.1), calls=%async_computation | async-start | bytes 1310720 | tf_op jit(solution)/shard_map/all_to_all | solution.py:22
  21.5 39.9 %copy-start.3 = (f32[7168]{0:T(1024)S(1)}, f32[7168]{0:T(1024)}, u32[]{:S(2)}) copy-start(f32[7168]{0:T(1024)} %param.18) | copy-start | bytes 86020
  21.6 1.4 %collective-permute-start = (bf16[512,128]{1,0:T(8,128)(2,1)S(1)}, bf16[512,128]{1,0:T(8,128)(2,1)S(1)}, u32[]{:S(2)}, u32[]{:S(2)}) collective-permute-start(bf16[512,128]{1,0:T(8,128)(2,1)S(1)} %bitcast.12), channel_id=1, source_target_pairs={{0,8},{8,0},{1,9},{9,1},{2,10},{10,2},{3,11},{11,3},{4,12},{12,4},... | collective-permute-start | bytes 393224 | tf_op jit(solution)/shard_map/ppermute | solution.py:26
  55.9 16.6 %all-to-all-start.2 = ((bf16[64,4,896]{2,1,0:T(4,128)(2,1)}), bf16[64,4,896]{2,1,0:T(4,128)(2,1)S(1)}, u32[]{:S(2)}, u32[]{:S(2)}) async-start(bf16[64,4,896]{2,1,0:T(4,128)(2,1)} %get-tuple-element.10), calls=%async_computation.2 | async-start | bytes 917504 | tf_op jit(solution)/shard_map/all_to_all | solution.py:22

commit v3 on v2

--- a/solution.py
+++ b/solution.py
@@ -11,8 +11,13 @@
 SMEM = pl.BlockSpec(memory_space=pltpu.SMEM)
 ANY = pl.BlockSpec(memory_space=pl.ANY)
 NOTES = 128
-SLABS = 8
-PIECES = 1
+SLABS = 2
+STAGED = 6
+EARLY = 4
+CHUNK = 256
+LOOK = False
+WINDOW = 16
+LOG2E = 1.4426950408889634
 LIMIT = 40 * 2**20
 f32 = jnp.float32
 bf16 = jnp.bfloat16
@@ -48,6 +53,7 @@
     route_scores,
     arrivals,
     small_arrivals,
+    query_arrivals,
 ):
     rows, feature, positions = cache.shape
     heads = query.shape[2]
@@ -59,32 +65,29 @@
         pltpu.make_async_copy(source, target, small_arrivals.at[place])
         for place, (source, target) in enumerate(
             (
-                (query_in, query),
                 (lengths_in, lengths),
                 (routes_in, routes),
                 (scores_in, route_scores),
             )
         )
     ]
-    copies = [
-        [
-            pltpu.make_async_copy(
-                cache.at[row, pl.ds(start, feature // PIECES)],
-                held.at[row, pl.ds(start, feature // PIECES)],
-                arrivals.at[row],
-            )
-            for start in range(0, feature, feature // PIECES)
-        ]
+    query_copies = [
+        pltpu.make_async_copy(query_in.at[row], query.at[row], query_arrivals.at[row])
         for row in range(rows)
     ]
-    for copy in small + sum(copies, []):
+    copies = [
+        pltpu.make_async_copy(cache.at[row], held.at[row], arrivals.at[row]) for row in range(rows)
+    ]
+    query_copies[0].start()
+    copies[0].start()
+    for copy in small + query_copies[1:] + copies[1:EARLY]:
         copy.start()
+    lane = lax.broadcasted_iota(jnp.int32, (heads, NOTES), 1)
+    expert = lax.broadcasted_iota(jnp.int32, (heads, NOTES), 0) // dev_count
+    position = lax.broadcasted_iota(jnp.int32, (1, positions), 1)
+    scale = feature**-0.5
     for copy in small:
         copy.wait()
-    lane = lax.broadcasted_iota(jnp.int32, (heads, NOTES), 1)
-    expert = lax.broadcasted_iota(jnp.int32, (heads, NOTES), 0) // dev_count
-    position = lax.broadcasted_iota(jnp.int32, (heads, positions), 1)
-    scale = feature**-0.5
     mixes = []
     for row in range(rows):
         total_score = route_scores[row, 0]
@@ -96,7 +99,10 @@
         mixes.append(2.5 * named / total_score)
 
     def raw_scores(row):
-        pltpu.make_async_copy(cache.at[row], held.at[row], arrivals.at[row]).wait()
+        query_copies[row].wait()
+        copies[row].wait()
+        for copy in copies[row + EARLY : row + EARLY + 1]:
+            copy.start()
         return lax.dot_general(
             query[row], held[row], (((0,), (0,)), ((), ())), preferred_element_type=f32
         )
@@ -104,19 +110,21 @@
     following = raw_scores(0)
     for row in range(rows):
         scores = following
-        if row + 1 < rows:
+        if LOOK and row + 1 < rows:
             following = raw_scores(row + 1)
         used = lengths[row] - dev * positions
-        scores = jnp.where(position < used, scores, -1e30)
+        scores = scores + jnp.where(position < used, 0.0, -1e30)
         top = jnp.max(scores, axis=1, keepdims=True)
-        weights = jnp.exp((scores - top) * scale)
-        total = jnp.sum(weights, axis=1, keepdims=True)
-        summed = lax.dot_general(
-            weights.astype(bf16),
-            held[row, :latent, :],
-            (((1,), (1,)), ((), ())),
-            preferred_element_type=f32,
-        )
+        total, summed = 0.0, 0.0
+        for start in range(0, positions, CHUNK):
+            weights = jnp.exp2((scores[:, start : start + CHUNK] - top) * (scale * LOG2E))
+            total = total + jnp.sum(weights, axis=1, keepdims=True)
+            summed = summed + lax.dot_general(
+                weights.astype(bf16),
+                held[row, :latent, start : start + CHUNK],
+                (((1,), (1,)), ((), ())),
+                preferred_element_type=f32,
+            )
         mean = summed / total
         log_total = jnp.where(used > 0, top * scale + jnp.log(total), -1e30)
         notes = jnp.zeros((heads, NOTES), f32)
@@ -129,6 +137,8 @@
             for tile in range(tiles):
                 joined[tile, target] = mean[source, tile * NOTES : (tile + 1) * NOTES]
             joined[tiles, target] = notes[source]
+        if not LOOK and row + 1 < rows:
+            following = raw_scores(row + 1)
     for tile in range(tiles + 1):
         columns = slice(tile * NOTES, (tile + 1) * NOTES)
         out[:, :, columns] = joined[tile].astype(bf16).reshape(out.shape[0], out.shape[1], NOTES)
@@ -143,7 +153,7 @@
     heads = queries.shape[2]
     return pl.pallas_call(
         attend_kernel,
-        out_shape=jax.ShapeDtypeStruct((heads // 2, 2 * rows, latent + NOTES), bf16),
+        out_shape=pltpu.VMEM((heads // 2, 2 * rows, latent + NOTES), bf16),
         in_specs=[ANY] * 5,
         out_specs=VMEM,
         scratch_shapes=[
@@ -154,7 +164,8 @@
             pltpu.SMEM(routes.shape, jnp.int32),
             pltpu.SMEM(route_scores.shape, f32),
             pltpu.SemaphoreType.DMA((rows,)),
-            pltpu.SemaphoreType.DMA((4,)),
+            pltpu.SemaphoreType.DMA((3,)),
+            pltpu.SemaphoreType.DMA((rows,)),
         ],
         compiler_params=pltpu.CompilerParams(vmem_limit_bytes=LIMIT),
         cost_estimate=pl.CostEstimate(
@@ -249,7 +260,7 @@
         residual_kernel,
         out_shape=(
             jax.ShapeDtypeStruct(arrived.shape[1:], f32),
-            jax.ShapeDtypeStruct(arrived.shape, bf16),
+            pltpu.VMEM(arrived.shape, bf16),
         ),
         in_specs=[VMEM, VMEM],
         out_specs=(VMEM, VMEM),
@@ -258,10 +269,42 @@
     )(arrived, hidden)
 
 
+def stage_kernel(after, gate_own, gate_other, up_own, up_other, out, arrivals):
+    share = out.shape[1]
+    copies = []
+    for place in range(out.shape[0]):
+        source = (gate_own, gate_other, up_own, up_other)[place % 4]
+        copies.append(
+            pltpu.make_async_copy(
+                source.at[pl.ds(place // 4 * share, share)], out.at[place], arrivals.at[place]
+            )
+        )
+    for copy in copies:
+        copy.start()
+    for copy in copies:
+        copy.wait()
+
+
+def stage(after, share, *weights):
+    return pl.pallas_call(
+        stage_kernel,
+        out_shape=pltpu.VMEM((STAGED, share, weights[0].shape[1]), bf16),
+        in_specs=[ANY] * 5,
+        out_specs=VMEM,
+        scratch_shapes=[pltpu.SemaphoreType.DMA((STAGED,))],
+        compiler_params=pltpu.CompilerParams(vmem_limit_bytes=4 * 2**20),
+        cost_estimate=pl.CostEstimate(
+            flops=0, bytes_accessed=4 * STAGED * share * weights[0].shape[1], transcendentals=0
+        ),
+        name="stage",
+    )(after, *[pinned(weight) for weight in weights])
+
+
 def experts_kernel(
     arrived,
     gain,
     coefficients,
+    staged,
     gate_own,
     gate_other,
     up_own,
@@ -278,37 +321,48 @@
     width = devs * share
     units = first.shape[2]
     core = lax.axis_index("core")
-    first_copies, second_copies = [], []
+    copies = []
     for dev in range(devs):
         band = pl.ds(dev * share, share)
         for place, source in enumerate((gate_own, gate_other, up_own, up_other)):
-            first_copies.append(
+            copies.append(
                 pltpu.make_async_copy(
                     source.at[band], first.at[place, band], first_arrivals.at[place, dev]
                 )
             )
-    for place, source in enumerate((down_own, down_other)):
-        for cut in range(SLABS):
-            band = pl.ds(cut * (units // SLABS), units // SLABS)
-            second_copies.append(
+    for dev in range(devs):
+        band = pl.ds(dev * share, share)
+        for place, source in enumerate((down_own, down_other)):
+            copies.append(
                 pltpu.make_async_copy(
-                    source.at[band], second.at[place, band], second_arrivals.at[place, cut]
+                    source.at[:, band], second.at[place, :, band], second_arrivals.at[place, dev]
                 )
             )
-    for copy in first_copies + second_copies:
-        copy.start()
+    copies = copies[STAGED:]
+    begun = [copy.start() for copy in copies[:WINDOW]]
+    arrived_count = 0
+
+    def receive(until):
+        nonlocal arrived_count
+        while arrived_count < until - STAGED:
+            copies[arrived_count].wait()
+            arrived_count += 1
+            if len(begun) < len(copies):
+                begun.append(copies[len(begun)].start())
+
     squares = jnp.zeros((pairs * rows, 1), f32)
     sums = [jnp.zeros((pairs * rows, units), f32) for _ in range(4)]
     for dev in range(devs):
         value = arrived[:, dev].astype(f32).reshape(pairs * rows, share)
         squares = squares + jnp.sum(value * value, axis=1, keepdims=True)
         value = (value * gain[dev : dev + 1, :]).astype(bf16)
+        receive(4 * dev + 4)
         for place in range(4):
-            first_copies[4 * dev + place].wait()
-        for place in range(4):
-            sums[place] = sums[place] + jnp.dot(
-                value, first[place, dev * share : (dev + 1) * share], preferred_element_type=f32
-            )
+            if 4 * dev + place < STAGED:
+                band = staged[4 * dev + place]
+            else:
+                band = first[place, dev * share : (dev + 1) * share]
+            sums[place] = sums[place] + jnp.dot(value, band, preferred_element_type=f32)
     factor = lax.rsqrt(squares * (1.0 / width) + 1e-06)
     activated = []
     for place in range(2):
@@ -316,32 +370,37 @@
         mix = jnp.where(core == place, coefficients[0], coefficients[1])
         mix = mix.reshape(pairs * rows, NOTES)[:, :1]
         activated.append((gate / (1.0 + jnp.exp(-gate)) * up * mix).astype(bf16))
-    for copy in second_copies:
-        copy.wait()
     for dev in range(devs):
+        receive(4 * devs + 2 * dev + 2)
         columns = slice(dev * share, (dev + 1) * share)
         value = jnp.dot(activated[0], second[0, :, columns], preferred_element_type=f32)
         value = value + jnp.dot(activated[1], second[1, :, columns], preferred_element_type=f32)
         part[:, dev] = value.astype(bf16).reshape(pairs, rows, share)
 
 
-def experts(arrived, gain, coefficients, *weights):
+def experts(arrived, gain, coefficients, staged, *weights):
     pairs, devs, rows, share = arrived.shape
     units = weights[0].shape[1]
     return pl.pallas_call(
         experts_kernel,
         out_shape=jax.ShapeDtypeStruct(arrived.shape, bf16),
-        in_specs=[VMEM] * 3 + [ANY] * 6,
+        in_specs=[VMEM] * 4 + [ANY] * 6,
         out_specs=VMEM,
         scratch_shapes=[
             pltpu.VMEM((4, devs * share, units), bf16),
             pltpu.VMEM((2, units, devs * share), bf16),
             pltpu.SemaphoreType.DMA((4, devs)),
-            pltpu.SemaphoreType.DMA((2, SLABS)),
+            pltpu.SemaphoreType.DMA((2, devs)),
         ],
         compiler_params=pltpu.CompilerParams(vmem_limit_bytes=LIMIT),
         name="experts",
-    )(arrived, gain, coefficients, *[pinned(weight) for weight in weights])
+    )(
+        arrived,
+        gain,
+        coefficients,
+        pinned(staged, pltpu.VMEM),
+        *[pinned(weight) for weight in weights],
+    )
 
 
 def finish_kernel(arrived, residual, out):
@@ -401,11 +460,13 @@
     )
     arrived = exchange(part.reshape(chips, rows, share))
     residual, copies = add_up(arrived, hidden)
+    staged = stage(residual, share, gate_weight, gate_other, up_weight, up_other)
     arrived = exchange(copies).reshape(pairs, devs, rows, share)
     part = experts(
         arrived,
         norm_gain.reshape(devs, share),
         coefficients,
+        staged,
         gate_weight,
         gate_other,
         up_weight,

time: 99.3 us -> 97.4 us (0.981)
  waiting for transfers between devices: 25.4 us -> 23.6 us
    all_to_all x2, waiting for transfers between devices: 24.1 us -> 22.3 us  [exchange(): lax.all_to_all(blocks, PLANE, split_axis=0, concat_axis=0, tiled=True)]
    pallas_call x1 -> x2, Pallas kernels: 8.85 us -> 10.5 us  [the longest x1 8.71 us: attend(): pl.pallas_call(attend_kernel, out_shape=pltpu.VMEM((heads // 2, 2 * rows,...]
    pallas_call x1, Pallas kernels: 9.21 us -> 7.62 us  [experts(): pl.pallas_call(experts_kernel, out_shape=jax.ShapeDtypeStruct(arrived.sha...]
  transfers between devices with their start and end apart: 7 -> 7, of which waited for: 3 -> 3; matrix products, arithmetic and copies ran while one was open for 0% -> 0% of each run, Pallas kernels for 12% -> 14%
where the time goes in v3:
time: 97.4 us; the launch traced here: 97 us
  blocking collectives  32.8 us (34%)
  waiting for transfers between devices  23.6 us (24%)
  Pallas kernels  22.1 us (23%)
  starting transfers between devices  18.3 us (19%)
    all_to_all x2, blocking collectives, exchange(): lax.all_to_all(blocks, PLANE, split_axis=0, concat_axis=0, tiled=True)  32.8 us
    all_to_all x2, waiting for transfers between devices, exchange(): lax.all_to_all(blocks, PLANE, split_axis=0, concat_axis=0, tiled=True)  22.3 us
    all_to_all x2, starting transfers between devices, exchange(): lax.all_to_all(blocks, PLANE, split_axis=0, concat_axis=0, tiled=True)  17.2 us
    pallas_call x1, Pallas kernels, attend(): pl.pallas_call(attend_kernel, out_shape=pltpu.VMEM((heads // 2, 2 * rows,...  8.71 us
    pallas_call x1, Pallas kernels, experts(): pl.pallas_call(experts_kernel, out_shape=jax.ShapeDtypeStruct(arrived.sha...  7.62 us
    pallas_call x1, Pallas kernels, project(): pl.pallas_call(project_kernel, out_shape=(jax.ShapeDtypeStruct((pairs, de...  2.16 us
  transfers between devices with their start and end apart: 7, of which 3 were waited for; matrix products, arithmetic and copies ran while one was open for 0% of the time, Pallas kernels for 14%

profile of v3, /device:TPU:0, one launch (start us, length us, event | category | flops | bytes accessed | tf_op | source)
XLA Modules:
  0.0 97.0 jit_solution(2142802275040209394)
XLA Ops:
  0.0 0.0 collective-permute-start.2
  0.0 0.5 collective-permute-start.3
  0.5 0.0 collective-permute-start.4
  0.5 0.5 collective-permute-start.1
  1.0 0.0 copy-start.1
  1.0 0.0 copy-start
  1.0 8.7 %attend.1 = bf16[64,8,640]{2,1,0:T(8,128)(2,1)} custom-call(s32[4]{0:T(128)} %lengths_in.1, s32[4,8]{1,0:T(4,128)} %routes_in.1, f32[4,8]{1,0:T(4,128)} %scores_in.1, bf16[4,576,128]{2,1,0:T(8,128)(2,1)} %bitcast.23, bf16[4,576,2048]{2,1,0:T(8,128)(2,1)} %bitcast.20), custom_call_target="tpu_custom_call" | custom-call | flops 2415919104 | bytes 9437184 | tf_op jit(solution)/shard_map/attend/pallas_call | solution.py:154
  9.7 0.0 copy-start.2
  9.8 11.6 %all-to-all-start = ((bf16[64,8,640]{2,1,0:T(8,128)(2,1)}), bf16[64,8,640]{2,1,0:T(8,128)(2,1)S(1)}, u32[]{:S(2)}, u32[]{:S(2)}) async-start(bf16[64,8,640]{2,1,0:T(8,128)(2,1)} %attend.1), calls=%async_computation | async-start | bytes 1310720 | tf_op jit(solution)/shard_map/all_to_all | solution.py:27
  21.4 0.0 copy-start.3
  21.4 0.0 copy-done.1
  21.4 0.1 collective-permute-start
  21.5 1.3 %collective-permute-done.up_other = bf16[512,128]{1,0:T(8,128)(2,1)S(1)} collective-permute-done((bf16[512,128]{1,0:T(8,128)(2,1)S(1)}, bf16[512,128]{1,0:T(8,128)(2,1)S(1)}, u32[]{:S(2)}, u32[]{:S(2)}) %collective-permute-start) | collective-permute-done | bytes 131104 | tf_op jit(solution)/shard_map/ppermute | solution.py:31
  22.9 13.1 %all-to-all-done.arrived = bf16[64,8,640]{2,1,0:T(8,128)(2,1)S(1)} async-done(((bf16[64,8,640]{2,1,0:T(8,128)(2,1)}), bf16[64,8,640]{2,1,0:T(8,128)(2,1)S(1)}, u32[]{:S(2)}, u32[]{:S(2)}) %all-to-all-start) | async-done | bytes 655392 | tf_op jit(solution)/shard_map/all_to_all | solution.py:27
  35.9 0.0 collective-permute-done.1.other_in
  35.9 0.0 copy-done
  35.9 2.2 %project.1 = (bf16[8,8,4,896]{3,2,1,0:T(4,128)(2,1)S(1)}, f32[2,8,4,128]{3,2,1,0:T(4,128)S(1)}) custom-call(bf16[64,8,640]{2,1,0:T(8,128)(2,1)S(1)} %all-to-all-done.arrived, bf16[512,128]{1,0:T(8,128)(2,1)S(1)} %bitcast.13, bf16[512,128]{1,0:T(8,128)(2,1)S(1)} %collective-permute-done.up_other, bf16[128,7168]{1,0:T(8,128)(2,1)S(1)} %copy-done, ...), custom_call_target="tpu_custom_call" | custom-call | tf_op jit(solution)/shard_map/project/pallas_call | solution.py:232
  38.1 16.4 %all_to_all.20.arrived = bf16[64,4,896]{2,1,0:T(4,128)(2,1)S(1)} all-to-all(bf16[64,4,896]{2,1,0:T(4,128)(2,1)S(1)} %bitcast.11), channel_id=1, replica_groups=mesh['pair'=8,'core'=2,'dev'=8] {'pair','dev'}, dimensions={0} | all-to-all | bytes 917504 | tf_op jit(solution)/shard_map/all_to_all | solution.py:27
  54.5 0.0 copy-done.2
  54.5 1.0 %residual.1 = (f32[4,896]{1,0:T(4,128)S(1)}, bf16[64,4,896]{2,1,0:T(4,128)(2,1)}) custom-call(bf16[64,4,896]{2,1,0:T(4,128)(2,1)S(1)} %all_to_all.20.arrived, bf16[4,7168]{1,0:T(4,128)(2,1)S(1)} %copy-done.2), custom_call_target="tpu_custom_call" | custom-call | tf_op jit(solution)/shard_map/residual/pallas_call | solution.py:259
  55.5 5.5 %all-to-all-start.2 = ((bf16[64,4,896]{2,1,0:T(4,128)(2,1)}), bf16[64,4,896]{2,1,0:T(4,128)(2,1)S(1)}, u32[]{:S(2)}, u32[]{:S(2)}) async-start(bf16[64,4,896]{2,1,0:T(4,128)(2,1)} %get-tuple-element.10), calls=%async_computation.2 | async-start | bytes 917504 | tf_op jit(solution)/shard_map/all_to_all | solution.py:27
  61.1 0.0 copy-done.3
  61.1 0.0 collective-permute-done.2.gate_other
  61.1 0.0 collective-permute-done.3.up_other
  61.1 1.8 %stage.1.staged = bf16[6,896,256]{2,1,0:T(8,128)(2,1)S(1)} custom-call(f32[4,896]{1,0:T(4,128)S(1)} %get-tuple-element.12.after.residual, bf16[7168,256]{1,0:T(8,128)(2,1)} %bitcast.15, bf16[7168,256]{1,0:T(8,128)(2,1)} %collective-permute-done.2.gate_other, bf16[7168,256]{1,0:T(8,128)(2,1)} %bitcast.18, bf16[7168,256]{1,0:T(8,128)(2,1)} %collective-permute-done.3.up_other), custom_call_target="tpu_custom_call" | custom-call | bytes 5505024 | tf_op jit(solution)/shard_map/stage/pallas_call | solution.py:289
  62.9 9.2 %all-to-all-done.2 = bf16[64,4,896]{2,1,0:T(4,128)(2,1)S(1)} async-done(((bf16[64,4,896]{2,1,0:T(4,128)(2,1)}), bf16[64,4,896]{2,1,0:T(4,128)(2,1)S(1)}, u32[]{:S(2)}, u32[]{:S(2)}) %all-to-all-start.2) | async-done | bytes 458784 | tf_op jit(solution)/shard_map/all_to_all | solution.py:27
  72.1 0.0 collective-permute-done.4.down_other
  72.1 7.6 %experts.1 = bf16[8,8,4,896]{3,2,1,0:T(4,128)(2,1)S(1)} custom-call(bf16[8,8,4,896]{3,2,1,0:T(4,128)(2,1)S(1)} %bitcast.9, f32[8,896]{1,0:T(8,128)S(1)} %reshape.14.gain, f32[2,8,4,128]{3,2,1,0:T(4,128)S(1)} %get-tuple-element.11.coefficients, bf16[6,896,256]{2,1,0:T(8,128)(2,1)S(1)} %stage.1.staged, bf16[7168,256]{1,0:T(8,128)(2,1)} %bitcast.16, ...), custom_call_target="tpu_custom_call" | custom-call | tf_op jit(solution)/shard_map/experts/pallas_call | solution.py:384
  79.8 16.4 %all_to_all.21.arrived = bf16[64,4,896]{2,1,0:T(4,128)(2,1)S(1)} all-to-all(bf16[64,4,896]{2,1,0:T(4,128)(2,1)S(1)} %bitcast.10), channel_id=1, replica_groups=mesh['pair'=8,'core'=2,'dev'=8] {'pair','dev'}, dimensions={0} | all-to-all | bytes 917504 | tf_op jit(solution)/shard_map/all_to_all | solution.py:27
  96.1 0.8 finish.1
  (1 shorter events, 0.0 us)
Async XLA Ops:
  0.0 61.1 %collective-permute-start.2 = (bf16[7168,256]{1,0:T(8,128)(2,1)}, bf16[7168,256]{1,0:T(8,128)(2,1)}, u32[]{:S(2)}, u32[]{:S(2)}) collective-permute-start(bf16[7168,256]{1,0:T(8,128)(2,1)} %bitcast.14), channel_id=1, source_target_pairs={{0,8},{8,0},{1,9},{9,1},{2,10},{10,2},{3,11},{11,3},{4,12},{12,4},... | collective-permute-start | bytes 11010056 | tf_op jit(solution)/shard_map/ppermute | solution.py:31
  0.0 61.1 %collective-permute-start.3 = (bf16[7168,256]{1,0:T(8,128)(2,1)}, bf16[7168,256]{1,0:T(8,128)(2,1)}, u32[]{:S(2)}, u32[]{:S(2)}) collective-permute-start(bf16[7168,256]{1,0:T(8,128)(2,1)} %bitcast.17), channel_id=1, source_target_pairs={{0,8},{8,0},{1,9},{9,1},{2,10},{10,2},{3,11},{11,3},{4,12},{12,4},... | collective-permute-start | bytes 11010056 | tf_op jit(solution)/shard_map/ppermute | solution.py:31
  0.5 71.6 %collective-permute-start.4 = (bf16[256,7168]{1,0:T(8,128)(2,1)}, bf16[256,7168]{1,0:T(8,128)(2,1)}, u32[]{:S(2)}, u32[]{:S(2)}) collective-permute-start(bf16[256,7168]{1,0:T(8,128)(2,1)} %bitcast.21), channel_id=1, source_target_pairs={{0,8},{8,0},{1,9},{9,1},{2,10},{10,2},{3,11},{11,3},{4,12},{12,4},... | collective-permute-start | bytes 11010056 | tf_op jit(solution)/shard_map/ppermute | solution.py:31
  0.5 35.4 %collective-permute-start.1 = (bf16[128,7168]{1,0:T(8,128)(2,1)}, bf16[128,7168]{1,0:T(8,128)(2,1)}, u32[]{:S(2)}, u32[]{:S(2)}) collective-permute-start(bf16[128,7168]{1,0:T(8,128)(2,1)} %out_own.1), channel_id=1, source_target_pairs={{0,8},{8,0},{1,9},{9,1},{2,10},{10,2},{3,11},{11,3},{4,12},{12,4},... | collective-permute-start | bytes 5505032 | tf_op jit(solution)/shard_map/ppermute | solution.py:31
  1.0 20.4 %copy-start.1 = (bf16[1,512,128]{2,1,0:T(8,128)(2,1)S(1)}, bf16[1,512,128]{2,1,0:T(8,128)(2,1)}, u32[]{:S(2)}) copy-start(bf16[1,512,128]{2,1,0:T(8,128)(2,1)} %param.16) | copy-start | bytes 393220
  1.0 34.9 %copy-start = (bf16[128,7168]{1,0:T(8,128)(2,1)S(1)}, bf16[128,7168]{1,0:T(8,128)(2,1)}, u32[]{:S(2)}) copy-start(bf16[128,7168]{1,0:T(8,128)(2,1)} %out_own.1) | copy-start | bytes 5505028
  9.7 44.8 %copy-start.2 = (bf16[4,7168]{1,0:T(4,128)(2,1)S(1)}, bf16[4,7168]{1,0:T(4,128)(2,1)}, u32[]{:S(2)}) copy-start(bf16[4,7168]{1,0:T(4,128)(2,1)} %hidden.1) | copy-start | bytes 172036
  9.8 26.1 %all-to-all-start = ((bf16[64,8,640]{2,1,0:T(8,128)(2,1)}), bf16[64,8,640]{2,1,0:T(8,128)(2,1)S(1)}, u32[]{:S(2)}, u32[]{:S(2)}) async-start(bf16[64,8,640]{2,1,0:T(8,128)(2,1)} %attend.1), calls=%async_computation | async-start | bytes 1310720 | tf_op jit(solution)/shard_map/all_to_all | solution.py:27
  21.4 39.7 %copy-start.3 = (f32[7168]{0:T(1024)S(1)}, f32[7168]{0:T(1024)}, u32[]{:S(2)}) copy-start(f32[7168]{0:T(1024)} %param.18) | copy-start | bytes 86020
  21.4 1.4 %collective-permute-start = (bf16[512,128]{1,0:T(8,128)(2,1)S(1)}, bf16[512,128]{1,0:T(8,128)(2,1)S(1)}, u32[]{:S(2)}, u32[]{:S(2)}) collective-permute-start(bf16[512,128]{1,0:T(8,128)(2,1)S(1)} %bitcast.12), channel_id=1, source_target_pairs={{0,8},{8,0},{1,9},{9,1},{2,10},{10,2},{3,11},{11,3},{4,12},{12,4},... | collective-permute-start | bytes 393224 | tf_op jit(solution)/shard_map/ppermute | solution.py:31
  55.5 16.6 %all-to-all-start.2 = ((bf16[64,4,896]{2,1,0:T(4,128)(2,1)}), bf16[64,4,896]{2,1,0:T(4,128)(2,1)S(1)}, u32[]{:S(2)}, u32[]{:S(2)}) async-start(bf16[64,4,896]{2,1,0:T(4,128)(2,1)} %get-tuple-element.10), calls=%async_computation.2 | async-start | bytes 917504 | tf_op jit(solution)/shard_map/all_to_all | solution.py:27

commit v4 on v3

--- a/solution.py
+++ b/solution.py
@@ -1,3 +1,5 @@
+import functools
+
 import jax
 import jax.numpy as jnp
 from jax import lax
@@ -78,9 +80,7 @@
     copies = [
         pltpu.make_async_copy(cache.at[row], held.at[row], arrivals.at[row]) for row in range(rows)
     ]
-    query_copies[0].start()
-    copies[0].start()
-    for copy in small + query_copies[1:] + copies[1:EARLY]:
+    for copy in query_copies[:1] + copies[:1] + small + query_copies[1:] + copies[1:]:
         copy.start()
     lane = lax.broadcasted_iota(jnp.int32, (heads, NOTES), 1)
     expert = lax.broadcasted_iota(jnp.int32, (heads, NOTES), 0) // dev_count
@@ -88,57 +88,57 @@
     scale = feature**-0.5
     for copy in small:
         copy.wait()
-    mixes = []
-    for row in range(rows):
+
+    def one_row(row, carry):
         total_score = route_scores[row, 0]
         for k in range(1, routes.shape[1]):
             total_score = total_score + route_scores[row, k]
         named = jnp.zeros((heads, NOTES), f32)
         for k in range(routes.shape[1]):
             named = jnp.where(expert == routes[row, k], route_scores[row, k], named)
-        mixes.append(2.5 * named / total_score)
-
-    def raw_scores(row):
-        query_copies[row].wait()
-        copies[row].wait()
-        for copy in copies[row + EARLY : row + EARLY + 1]:
-            copy.start()
-        return lax.dot_general(
-            query[row], held[row], (((0,), (0,)), ((), ())), preferred_element_type=f32
-        )
-
-    following = raw_scores(0)
-    for row in range(rows):
-        scores = following
-        if LOOK and row + 1 < rows:
-            following = raw_scores(row + 1)
+        mix = 2.5 * named / total_score
         used = lengths[row] - dev * positions
-        scores = scores + jnp.where(position < used, 0.0, -1e30)
-        top = jnp.max(scores, axis=1, keepdims=True)
-        total, summed = 0.0, 0.0
-        for start in range(0, positions, CHUNK):
-            weights = jnp.exp2((scores[:, start : start + CHUNK] - top) * (scale * LOG2E))
-            total = total + jnp.sum(weights, axis=1, keepdims=True)
-            summed = summed + lax.dot_general(
-                weights.astype(bf16),
-                held[row, :latent, start : start + CHUNK],
-                (((1,), (1,)), ((), ())),
-                preferred_element_type=f32,
+        pltpu.make_async_copy(query_in.at[row], query.at[row], query_arrivals.at[row]).wait()
+        pltpu.make_async_copy(cache.at[row], held.at[row], arrivals.at[row]).wait()
+
+        def store(mean, log_total):
+            notes = jnp.zeros((heads, NOTES), f32)
+            for place, part in enumerate(thirds(log_total) + thirds(mix)):
+                notes = jnp.where(lane == place, part, notes)
+            for group in range(heads // 8):
+                pair, core = group // 2, group % 2
+                target = pl.ds(pair * 64 + core * rows + row, 8, stride=8)
+                source = slice(group * 8, group * 8 + 8)
+                for tile in range(tiles):
+                    joined[tile, target] = mean[source, tile * NOTES : (tile + 1) * NOTES]
+                joined[tiles, target] = notes[source]
+
+        @pl.when(used > 0)
+        def _():
+            scores = lax.dot_general(
+                query[row], held[row], (((0,), (0,)), ((), ())), preferred_element_type=f32
             )
-        mean = summed / total
-        log_total = jnp.where(used > 0, top * scale + jnp.log(total), -1e30)
-        notes = jnp.zeros((heads, NOTES), f32)
-        for place, part in enumerate(thirds(log_total) + thirds(mixes[row])):
-            notes = jnp.where(lane == place, part, notes)
-        for group in range(heads // 8):
-            pair, core = group // 2, group % 2
-            target = pl.ds(pair * 64 + core * rows + row, 8, stride=8)
-            source = slice(group * 8, group * 8 + 8)
-            for tile in range(tiles):
-                joined[tile, target] = mean[source, tile * NOTES : (tile + 1) * NOTES]
-            joined[tiles, target] = notes[source]
-        if not LOOK and row + 1 < rows:
-            following = raw_scores(row + 1)
+            scores = scores + jnp.where(position < used, 0.0, -1e30)
+            top = jnp.max(scores, axis=1, keepdims=True)
+            total, summed = 0.0, 0.0
+            for start in range(0, positions, CHUNK):
+                weights = jnp.exp2((scores[:, start : start + CHUNK] - top) * (scale * LOG2E))
+                total = total + jnp.sum(weights, axis=1, keepdims=True)
+                summed = summed + lax.dot_general(
+                    weights.astype(bf16),
+                    held[row, :latent, start : start + CHUNK],
+                    (((1,), (1,)), ((), ())),
+                    preferred_element_type=f32,
+                )
+            store(summed / total, top * scale + jnp.log(total))
+
+        @pl.when(used <= 0)
+        def _():
+            store(jnp.zeros((heads, latent), f32), jnp.full((heads, 1), -1e30, f32))
+
+        return carry
+
+    lax.fori_loop(0, rows, one_row, 0)
     for tile in range(tiles + 1):
         columns = slice(tile * NOTES, (tile + 1) * NOTES)
         out[:, :, columns] = joined[tile].astype(bf16).reshape(out.shape[0], out.shape[1], NOTES)
@@ -217,18 +217,19 @@
         return picked.reshape(pairs * rows, -1).astype(bf16)
 
     own, other = head(up_own, True), head(up_other, False)
+    weight = out_own.reshape(out_other.shape)
     for copy in copies:
         copy.wait()
     for dev in range(devs):
         columns = slice(dev * share, (dev + 1) * share)
-        value = jnp.dot(own, out_own[:, columns], preferred_element_type=f32)
+        value = jnp.dot(own, weight[:, columns], preferred_element_type=f32)
         value = value + jnp.dot(other, out_other[:, columns], preferred_element_type=f32)
         part[:, dev] = value.astype(bf16).reshape(pairs, rows, share)
 
 
 def project(arrived, up_own, up_other, out_own, out_other, pairs, devs):
     rows = arrived.shape[1] // 2
-    width = out_own.shape[1]
+    width = out_other.shape[1]
     return pl.pallas_call(
         project_kernel,
         out_shape=(
@@ -243,7 +244,7 @@
         ],
         compiler_params=pltpu.CompilerParams(vmem_limit_bytes=LIMIT),
         name="project",
-    )(arrived, up_own, up_other, out_own, pinned(out_other))
+    )(arrived, up_own, up_other, pinned(out_own, pltpu.VMEM), pinned(out_other))
 
 
 def residual_kernel(arrived, hidden, residual, copies):
@@ -269,14 +270,14 @@
     )(arrived, hidden)
 
 
-def stage_kernel(after, gate_own, gate_other, up_own, up_other, out, arrivals):
+def stage_kernel(bands, after, *refs):
+    sources, out, arrivals = refs[:-2], refs[-2], refs[-1]
     share = out.shape[1]
     copies = []
-    for place in range(out.shape[0]):
-        source = (gate_own, gate_other, up_own, up_other)[place % 4]
+    for place, (source, band) in enumerate(bands):
         copies.append(
             pltpu.make_async_copy(
-                source.at[pl.ds(place // 4 * share, share)], out.at[place], arrivals.at[place]
+                sources[source].at[pl.ds(band * share, share)], out.at[place], arrivals.at[place]
             )
         )
     for copy in copies:
@@ -285,16 +286,17 @@
         copy.wait()
 
 
-def stage(after, share, *weights):
+def stage(after, share, bands, *weights):
+    width = weights[0].shape[1]
     return pl.pallas_call(
-        stage_kernel,
-        out_shape=pltpu.VMEM((STAGED, share, weights[0].shape[1]), bf16),
-        in_specs=[ANY] * 5,
+        functools.partial(stage_kernel, bands),
+        out_shape=pltpu.VMEM((len(bands), share, width), bf16),
+        in_specs=[ANY] * (len(weights) + 1),
         out_specs=VMEM,
-        scratch_shapes=[pltpu.SemaphoreType.DMA((STAGED,))],
+        scratch_shapes=[pltpu.SemaphoreType.DMA((len(bands),))],
         compiler_params=pltpu.CompilerParams(vmem_limit_bytes=4 * 2**20),
         cost_estimate=pl.CostEstimate(
-            flops=0, bytes_accessed=4 * STAGED * share * weights[0].shape[1], transcendentals=0
+            flops=0, bytes_accessed=4 * len(bands) * share * width, transcendentals=0
         ),
         name="stage",
     )(after, *[pinned(weight) for weight in weights])
@@ -455,12 +457,15 @@
         jnp.swapaxes(latent_cache, 1, 2),
         latent,
     )
+    half = output_weight.shape[0] // 2
+    output_own = stage(parts, half, ((0, 0), (0, 1)), output_weight)
     part, coefficients = project(
-        exchange(parts), value_up, value_other, output_weight, output_other, pairs, devs
+        exchange(parts), value_up, value_other, output_own, output_other, pairs, devs
     )
     arrived = exchange(part.reshape(chips, rows, share))
     residual, copies = add_up(arrived, hidden)
-    staged = stage(residual, share, gate_weight, gate_other, up_weight, up_other)
+    bands = tuple((place % 4, place // 4) for place in range(STAGED))
+    staged = stage(residual, share, bands, gate_weight, gate_other, up_weight, up_other)
     arrived = exchange(copies).reshape(pairs, devs, rows, share)
     part = experts(
         arrived,

time: 97.4 us -> 95.8 us (0.984)
  starting transfers between devices: 18.3 us -> 16.1 us
  Pallas kernels: 22.1 us -> 23.6 us
  waiting for transfers between devices: 23.6 us -> 22.6 us
    all_to_all x2, starting transfers between devices: 17.2 us -> 14.9 us  [exchange(): lax.all_to_all(blocks, PLANE, split_axis=0, concat_axis=0, tiled=True)]
    pallas_call x1 -> x2, Pallas kernels: 1.77 us -> 3.24 us  [stage(): pl.pallas_call(functools.partial(stage_kernel, bands), out_shape=pltpu.VM...]
    ppermute x5, waiting for transfers between devices: 1.35 us -> 0.01 us  [other_core(): return lax.ppermute(value, 'core', [(0, 1), (1, 0)])]
  transfers between devices with their start and end apart: 7 -> 7, of which waited for: 3 -> 2; matrix products, arithmetic and copies ran while one was open for 0% -> 0% of each run, Pallas kernels for 14% -> 16%
where the time goes in v4:
time: 95.8 us; the launch traced here: 95.5 us
  blocking collectives  33.1 us (35%)
  Pallas kernels  23.6 us (25%)
  waiting for transfers between devices  22.6 us (24%)
  starting transfers between devices  16.1 us (17%)
    all_to_all x2, blocking collectives, exchange(): lax.all_to_all(blocks, PLANE, split_axis=0, concat_axis=0, tiled=True)  33.1 us
    all_to_all x2, waiting for transfers between devices, exchange(): lax.all_to_all(blocks, PLANE, split_axis=0, concat_axis=0, tiled=True)  22.5 us
    all_to_all x2, starting transfers between devices, exchange(): lax.all_to_all(blocks, PLANE, split_axis=0, concat_axis=0, tiled=True)  14.9 us
    pallas_call x1, Pallas kernels, attend(): pl.pallas_call(attend_kernel, out_shape=pltpu.VMEM((heads // 2, 2 * rows,...  8.8 us
    pallas_call x1, Pallas kernels, experts(): pl.pallas_call(experts_kernel, out_shape=jax.ShapeDtypeStruct(arrived.sha...  7.62 us
    pallas_call x2, Pallas kernels, stage(): pl.pallas_call(functools.partial(stage_kernel, bands), out_shape=pltpu.VM...  3.24 us
    pallas_call x1, Pallas kernels, project(): pl.pallas_call(project_kernel, out_shape=(jax.ShapeDtypeStruct((pairs, de...  2.16 us
  transfers between devices with their start and end apart: 7, of which 2 were waited for; matrix products, arithmetic and copies ran while one was open for 0% of the time, Pallas kernels for 16%

profile of v4, /device:TPU:0, one launch (start us, length us, event | category | flops | bytes accessed | tf_op | source)
XLA Modules:
  0.0 95.5 jit_solution(3666127557546383357)
XLA Ops:
  0.0 0.0 collective-permute-start.2
  0.0 0.5 collective-permute-start.3
  0.5 0.0 collective-permute-start.4
  0.5 0.5 collective-permute-start.1
  1.0 0.0 copy-start
  1.0 8.8 %attend.1.after = bf16[64,8,640]{2,1,0:T(8,128)(2,1)} custom-call(s32[4]{0:T(128)} %lengths_in.1, s32[4,8]{1,0:T(4,128)} %routes_in.1, f32[4,8]{1,0:T(4,128)} %scores_in.1, bf16[4,576,128]{2,1,0:T(8,128)(2,1)} %bitcast.23, bf16[4,576,2048]{2,1,0:T(8,128)(2,1)} %bitcast.20), custom_call_target="tpu_custom_call" | custom-call | flops 2415919104 | bytes 9437184 | tf_op jit(solution)/shard_map/attend/pallas_call | solution.py:154
  9.8 9.7 %all-to-all-start = ((bf16[64,8,640]{2,1,0:T(8,128)(2,1)}), bf16[64,8,640]{2,1,0:T(8,128)(2,1)S(1)}, u32[]{:S(2)}, u32[]{:S(2)}) async-start(bf16[64,8,640]{2,1,0:T(8,128)(2,1)} %attend.1.after), calls=%async_computation | async-start | bytes 1310720 | tf_op jit(solution)/shard_map/all_to_all | solution.py:29
  19.6 0.0 copy-done
  19.6 0.1 collective-permute-start
  19.7 1.5 %stage.2.out_own = bf16[2,64,7168]{2,1,0:T(8,128)(2,1)S(1)} custom-call(bf16[64,8,640]{2,1,0:T(8,128)(2,1)} %attend.1.after, bf16[128,7168]{1,0:T(8,128)(2,1)} %refs_0_.1), custom_call_target="tpu_custom_call" | custom-call | bytes 3670016 | tf_op jit(solution)/shard_map/stage/pallas_call | solution.py:291
  21.2 0.0 copy-start.1
  21.2 0.0 copy-start.2
  21.2 0.0 collective-permute-done.up_other
  21.2 13.1 %all-to-all-done.arrived = bf16[64,8,640]{2,1,0:T(8,128)(2,1)S(1)} async-done(((bf16[64,8,640]{2,1,0:T(8,128)(2,1)}), bf16[64,8,640]{2,1,0:T(8,128)(2,1)S(1)}, u32[]{:S(2)}, u32[]{:S(2)}) %all-to-all-start) | async-done | bytes 655392 | tf_op jit(solution)/shard_map/all_to_all | solution.py:29
  34.3 0.0 collective-permute-done.1.other_in
  34.3 2.2 %project.1 = (bf16[8,8,4,896]{3,2,1,0:T(4,128)(2,1)S(1)}, f32[2,8,4,128]{3,2,1,0:T(4,128)S(1)}) custom-call(bf16[64,8,640]{2,1,0:T(8,128)(2,1)S(1)} %all-to-all-done.arrived, bf16[512,128]{1,0:T(8,128)(2,1)S(1)} %bitcast.13, bf16[512,128]{1,0:T(8,128)(2,1)S(1)} %collective-permute-done.up_other, bf16[2,64,7168]{2,1,0:T(8,128)(2,1)S(1)} %stage.2.out_own, ...), custom_call_target="tpu_custom_call" | custom-call | tf_op jit(solution)/shard_map/project/pallas_call | solution.py:233
  36.5 16.7 %all_to_all.20.arrived = bf16[64,4,896]{2,1,0:T(4,128)(2,1)S(1)} all-to-all(bf16[64,4,896]{2,1,0:T(4,128)(2,1)S(1)} %bitcast.11), channel_id=1, replica_groups=mesh['pair'=8,'core'=2,'dev'=8] {'pair','dev'}, dimensions={0} | all-to-all | bytes 917504 | tf_op jit(solution)/shard_map/all_to_all | solution.py:29
  53.2 0.0 copy-done.1
  53.2 1.0 %residual.1 = (f32[4,896]{1,0:T(4,128)S(1)}, bf16[64,4,896]{2,1,0:T(4,128)(2,1)}) custom-call(bf16[64,4,896]{2,1,0:T(4,128)(2,1)S(1)} %all_to_all.20.arrived, bf16[4,7168]{1,0:T(4,128)(2,1)S(1)} %copy-done.1), custom_call_target="tpu_custom_call" | custom-call | tf_op jit(solution)/shard_map/residual/pallas_call | solution.py:260
  54.2 5.2 %all-to-all-start.2 = ((bf16[64,4,896]{2,1,0:T(4,128)(2,1)}), bf16[64,4,896]{2,1,0:T(4,128)(2,1)S(1)}, u32[]{:S(2)}, u32[]{:S(2)}) async-start(bf16[64,4,896]{2,1,0:T(4,128)(2,1)} %get-tuple-element.10), calls=%async_computation.2 | async-start | bytes 917504 | tf_op jit(solution)/shard_map/all_to_all | solution.py:29
  59.4 0.0 copy-done.2
  59.4 0.0 collective-permute-done.2.refs_1_.gate_other
  59.5 0.0 collective-permute-done.3.refs_3_.up_other
  59.5 1.8 %stage.3.staged = bf16[6,896,256]{2,1,0:T(8,128)(2,1)S(1)} custom-call(f32[4,896]{1,0:T(4,128)S(1)} %get-tuple-element.12.after.residual, bf16[7168,256]{1,0:T(8,128)(2,1)} %bitcast.15, bf16[7168,256]{1,0:T(8,128)(2,1)} %collective-permute-done.2.refs_1_.gate_other, bf16[7168,256]{1,0:T(8,128)(2,1)} %bitcast.18, ...), custom_call_target="tpu_custom_call" | custom-call | bytes 5505024 | tf_op jit(solution)/shard_map/stage/pallas_call | solution.py:291
  61.2 9.4 %all-to-all-done.2 = bf16[64,4,896]{2,1,0:T(4,128)(2,1)S(1)} async-done(((bf16[64,4,896]{2,1,0:T(4,128)(2,1)}), bf16[64,4,896]{2,1,0:T(4,128)(2,1)S(1)}, u32[]{:S(2)}, u32[]{:S(2)}) %all-to-all-start.2) | async-done | bytes 458784 | tf_op jit(solution)/shard_map/all_to_all | solution.py:29
  70.7 0.0 collective-permute-done.4.down_other
  70.7 7.6 %experts.1 = bf16[8,8,4,896]{3,2,1,0:T(4,128)(2,1)S(1)} custom-call(bf16[8,8,4,896]{3,2,1,0:T(4,128)(2,1)S(1)} %bitcast.9, f32[8,896]{1,0:T(8,128)S(1)} %reshape.14.gain, f32[2,8,4,128]{3,2,1,0:T(4,128)S(1)} %get-tuple-element.11.coefficients, bf16[6,896,256]{2,1,0:T(8,128)(2,1)S(1)} %stage.3.staged, bf16[7168,256]{1,0:T(8,128)(2,1)} %bitcast.16, ...), custom_call_target="tpu_custom_call" | custom-call | tf_op jit(solution)/shard_map/experts/pallas_call | solution.py:386
  78.3 16.4 %all_to_all.21.arrived = bf16[64,4,896]{2,1,0:T(4,128)(2,1)S(1)} all-to-all(bf16[64,4,896]{2,1,0:T(4,128)(2,1)S(1)} %bitcast.10), channel_id=1, replica_groups=mesh['pair'=8,'core'=2,'dev'=8] {'pair','dev'}, dimensions={0} | all-to-all | bytes 917504 | tf_op jit(solution)/shard_map/all_to_all | solution.py:29
  94.7 0.8 finish.1
  (1 shorter events, 0.0 us)
Async XLA Ops:
  0.0 59.4 %collective-permute-start.2 = (bf16[7168,256]{1,0:T(8,128)(2,1)}, bf16[7168,256]{1,0:T(8,128)(2,1)}, u32[]{:S(2)}, u32[]{:S(2)}) collective-permute-start(bf16[7168,256]{1,0:T(8,128)(2,1)} %bitcast.14), channel_id=1, source_target_pairs={{0,8},{8,0},{1,9},{9,1},{2,10},{10,2},{3,11},{11,3},{4,12},{12,4},... | collective-permute-start | bytes 11010056 | tf_op jit(solution)/shard_map/ppermute | solution.py:33
  0.0 59.5 %collective-permute-start.3 = (bf16[7168,256]{1,0:T(8,128)(2,1)}, bf16[7168,256]{1,0:T(8,128)(2,1)}, u32[]{:S(2)}, u32[]{:S(2)}) collective-permute-start(bf16[7168,256]{1,0:T(8,128)(2,1)} %bitcast.17), channel_id=1, source_target_pairs={{0,8},{8,0},{1,9},{9,1},{2,10},{10,2},{3,11},{11,3},{4,12},{12,4},... | collective-permute-start | bytes 11010056 | tf_op jit(solution)/shard_map/ppermute | solution.py:33
  0.5 70.1 %collective-permute-start.4 = (bf16[256,7168]{1,0:T(8,128)(2,1)}, bf16[256,7168]{1,0:T(8,128)(2,1)}, u32[]{:S(2)}, u32[]{:S(2)}) collective-permute-start(bf16[256,7168]{1,0:T(8,128)(2,1)} %bitcast.21), channel_id=1, source_target_pairs={{0,8},{8,0},{1,9},{9,1},{2,10},{10,2},{3,11},{11,3},{4,12},{12,4},... | collective-permute-start | bytes 11010056 | tf_op jit(solution)/shard_map/ppermute | solution.py:33
  0.5 33.8 %collective-permute-start.1 = (bf16[128,7168]{1,0:T(8,128)(2,1)}, bf16[128,7168]{1,0:T(8,128)(2,1)}, u32[]{:S(2)}, u32[]{:S(2)}) collective-permute-start(bf16[128,7168]{1,0:T(8,128)(2,1)} %refs_0_.1), channel_id=1, source_target_pairs={{0,8},{8,0},{1,9},{9,1},{2,10},{10,2},{3,11},{11,3},{4,12},{12,4},... | collective-permute-start | bytes 5505032 | tf_op jit(solution)/shard_map/ppermute | solution.py:33
  1.0 18.6 %copy-start = (bf16[1,512,128]{2,1,0:T(8,128)(2,1)S(1)}, bf16[1,512,128]{2,1,0:T(8,128)(2,1)}, u32[]{:S(2)}) copy-start(bf16[1,512,128]{2,1,0:T(8,128)(2,1)} %param.16) | copy-start | bytes 393220
  9.8 24.5 %all-to-all-start = ((bf16[64,8,640]{2,1,0:T(8,128)(2,1)}), bf16[64,8,640]{2,1,0:T(8,128)(2,1)S(1)}, u32[]{:S(2)}, u32[]{:S(2)}) async-start(bf16[64,8,640]{2,1,0:T(8,128)(2,1)} %attend.1.after), calls=%async_computation | async-start | bytes 1310720 | tf_op jit(solution)/shard_map/all_to_all | solution.py:29
  19.6 1.6 %collective-permute-start = (bf16[512,128]{1,0:T(8,128)(2,1)S(1)}, bf16[512,128]{1,0:T(8,128)(2,1)S(1)}, u32[]{:S(2)}, u32[]{:S(2)}) collective-permute-start(bf16[512,128]{1,0:T(8,128)(2,1)S(1)} %bitcast.12), channel_id=1, source_target_pairs={{0,8},{8,0},{1,9},{9,1},{2,10},{10,2},{3,11},{11,3},{4,12},{12,4},... | collective-permute-start | bytes 393224 | tf_op jit(solution)/shard_map/ppermute | solution.py:33
  21.2 32.0 %copy-start.1 = (bf16[4,7168]{1,0:T(4,128)(2,1)S(1)}, bf16[4,7168]{1,0:T(4,128)(2,1)}, u32[]{:S(2)}) copy-start(bf16[4,7168]{1,0:T(4,128)(2,1)} %hidden.1) | copy-start | bytes 172036
  21.2 38.2 %copy-start.2 = (f32[7168]{0:T(1024)S(1)}, f32[7168]{0:T(1024)}, u32[]{:S(2)}) copy-start(f32[7168]{0:T(1024)} %param.18) | copy-start | bytes 86020
  54.2 16.4 %all-to-all-start.2 = ((bf16[64,4,896]{2,1,0:T(4,128)(2,1)}), bf16[64,4,896]{2,1,0:T(4,128)(2,1)S(1)}, u32[]{:S(2)}, u32[]{:S(2)}) async-start(bf16[64,4,896]{2,1,0:T(4,128)(2,1)} %get-tuple-element.10), calls=%async_computation.2 | async-start | bytes 917504 | tf_op jit(solution)/shard_map/all_to_all | solution.py:29

commit v5 on v4

--- a/solution.py
+++ b/solution.py
@@ -178,7 +178,7 @@
 
 
 def project_kernel(
-    arrived, up_own, up_other, out_own, other_in, part, coefficients, out_other, arrivals
+    arrived, up_own, up_other, out_own, other_in, part, coefficients, out_other, held, arrivals
 ):
     copies = []
     for cut in range(SLABS):
@@ -218,12 +218,16 @@
 
     own, other = head(up_own, True), head(up_other, False)
     weight = out_own.reshape(out_other.shape)
+    for dev in range(devs):
+        columns = slice(dev * share, (dev + 1) * share)
+        held[:, columns] = jnp.dot(own, weight[:, columns], preferred_element_type=f32)
     for copy in copies:
         copy.wait()
     for dev in range(devs):
         columns = slice(dev * share, (dev + 1) * share)
-        value = jnp.dot(own, weight[:, columns], preferred_element_type=f32)
-        value = value + jnp.dot(other, out_other[:, columns], preferred_element_type=f32)
+        value = held[:, columns] + jnp.dot(
+            other, out_other[:, columns], preferred_element_type=f32
+        )
         part[:, dev] = value.astype(bf16).reshape(pairs, rows, share)
 
 
@@ -240,6 +244,7 @@
         out_specs=(VMEM, VMEM),
         scratch_shapes=[
             pltpu.VMEM(out_other.shape, bf16),
+            pltpu.VMEM((pairs * rows, width), f32),
             pltpu.SemaphoreType.DMA((SLABS,)),
         ],
         compiler_params=pltpu.CompilerParams(vmem_limit_bytes=LIMIT),

time: 95.8 us -> 95.1 us (level)
  waiting for transfers between devices: 22.6 us -> 20.7 us
  starting transfers between devices: 16.1 us -> 18 us
    all_to_all x2, starting transfers between devices: 14.9 us -> 16.9 us  [exchange(): lax.all_to_all(blocks, PLANE, split_axis=0, concat_axis=0, tiled=True)]
    all_to_all x2, waiting for transfers between devices: 22.5 us -> 20.6 us  [exchange(): lax.all_to_all(blocks, PLANE, split_axis=0, concat_axis=0, tiled=True)]
where the time goes in v5:
time: 95.1 us; the launch traced here: 95 us
  blocking collectives  32.8 us (34%)
  Pallas kernels  23.4 us (25%)
  waiting for transfers between devices  20.7 us (22%)
  starting transfers between devices  18 us (19%)
    all_to_all x2, blocking collectives, exchange(): lax.all_to_all(blocks, PLANE, split_axis=0, concat_axis=0, tiled=True)  32.8 us
    all_to_all x2, waiting for transfers between devices, exchange(): lax.all_to_all(blocks, PLANE, split_axis=0, concat_axis=0, tiled=True)  20.6 us
    all_to_all x2, starting transfers between devices, exchange(): lax.all_to_all(blocks, PLANE, split_axis=0, concat_axis=0, tiled=True)  16.9 us
    pallas_call x1, Pallas kernels, attend(): pl.pallas_call(attend_kernel, out_shape=pltpu.VMEM((heads // 2, 2 * rows,...  8.8 us
    pallas_call x1, Pallas kernels, experts(): pl.pallas_call(experts_kernel, out_shape=jax.ShapeDtypeStruct(arrived.sha...  7.62 us
    pallas_call x2, Pallas kernels, stage(): pl.pallas_call(functools.partial(stage_kernel, bands), out_shape=pltpu.VM...  3.24 us
    pallas_call x1, Pallas kernels, project(): pl.pallas_call(project_kernel, out_shape=(jax.ShapeDtypeStruct((pairs, de...  1.95 us
  transfers between devices with their start and end apart: 7, of which 2 were waited for; matrix products, arithmetic and copies ran while one was open for 0% of the time, Pallas kernels for 16%

profile of v5, /device:TPU:0, one launch (start us, length us, event | category | flops | bytes accessed | tf_op | source)
XLA Modules:
  0.0 95.0 jit_solution(13931820942168803511)
XLA Ops:
  0.0 0.0 collective-permute-start.2
  0.0 0.5 collective-permute-start.3
  0.5 0.0 collective-permute-start.4
  0.5 0.5 collective-permute-start.1
  1.0 0.0 copy-start
  1.0 8.8 %attend.1.after = bf16[64,8,640]{2,1,0:T(8,128)(2,1)} custom-call(s32[4]{0:T(128)} %lengths_in.1, s32[4,8]{1,0:T(4,128)} %routes_in.1, f32[4,8]{1,0:T(4,128)} %scores_in.1, bf16[4,576,128]{2,1,0:T(8,128)(2,1)} %bitcast.23, bf16[4,576,2048]{2,1,0:T(8,128)(2,1)} %bitcast.20), custom_call_target="tpu_custom_call" | custom-call | flops 2415919104 | bytes 9437184 | tf_op jit(solution)/shard_map/attend/pallas_call | solution.py:154
  9.8 11.5 %all-to-all-start = ((bf16[64,8,640]{2,1,0:T(8,128)(2,1)}), bf16[64,8,640]{2,1,0:T(8,128)(2,1)S(1)}, u32[]{:S(2)}, u32[]{:S(2)}) async-start(bf16[64,8,640]{2,1,0:T(8,128)(2,1)} %attend.1.after), calls=%async_computation | async-start | bytes 1310720 | tf_op jit(solution)/shard_map/all_to_all | solution.py:29
  21.3 0.0 copy-done
  21.4 0.1 collective-permute-start
  21.4 1.5 %stage.2.out_own = bf16[2,64,7168]{2,1,0:T(8,128)(2,1)S(1)} custom-call(bf16[64,8,640]{2,1,0:T(8,128)(2,1)} %attend.1.after, bf16[128,7168]{1,0:T(8,128)(2,1)} %refs_0_.1), custom_call_target="tpu_custom_call" | custom-call | bytes 3670016 | tf_op jit(solution)/shard_map/stage/pallas_call | solution.py:296
  22.9 0.0 copy-start.1
  22.9 0.0 copy-start.2
  23.0 0.0 collective-permute-done.up_other
  23.0 11.2 %all-to-all-done.arrived = bf16[64,8,640]{2,1,0:T(8,128)(2,1)S(1)} async-done(((bf16[64,8,640]{2,1,0:T(8,128)(2,1)}), bf16[64,8,640]{2,1,0:T(8,128)(2,1)S(1)}, u32[]{:S(2)}, u32[]{:S(2)}) %all-to-all-start) | async-done | bytes 655392 | tf_op jit(solution)/shard_map/all_to_all | solution.py:29
  34.2 0.0 collective-permute-done.1.other_in
  34.2 2.0 %project.1 = (bf16[8,8,4,896]{3,2,1,0:T(4,128)(2,1)S(1)}, f32[2,8,4,128]{3,2,1,0:T(4,128)S(1)}) custom-call(bf16[64,8,640]{2,1,0:T(8,128)(2,1)S(1)} %all-to-all-done.arrived, bf16[512,128]{1,0:T(8,128)(2,1)S(1)} %bitcast.13, bf16[512,128]{1,0:T(8,128)(2,1)S(1)} %collective-permute-done.up_other, bf16[2,64,7168]{2,1,0:T(8,128)(2,1)S(1)} %stage.2.out_own, ...), custom_call_target="tpu_custom_call" | custom-call | tf_op jit(solution)/shard_map/project/pallas_call | solution.py:237
  36.2 16.4 %all_to_all.20.arrived = bf16[64,4,896]{2,1,0:T(4,128)(2,1)S(1)} all-to-all(bf16[64,4,896]{2,1,0:T(4,128)(2,1)S(1)} %bitcast.11), channel_id=1, replica_groups=mesh['pair'=8,'core'=2,'dev'=8] {'pair','dev'}, dimensions={0} | all-to-all | bytes 917504 | tf_op jit(solution)/shard_map/all_to_all | solution.py:29
  52.6 0.0 copy-done.1
  52.6 1.0 %residual.1 = (f32[4,896]{1,0:T(4,128)S(1)}, bf16[64,4,896]{2,1,0:T(4,128)(2,1)}) custom-call(bf16[64,4,896]{2,1,0:T(4,128)(2,1)S(1)} %all_to_all.20.arrived, bf16[4,7168]{1,0:T(4,128)(2,1)S(1)} %copy-done.1), custom_call_target="tpu_custom_call" | custom-call | tf_op jit(solution)/shard_map/residual/pallas_call | solution.py:265
  53.6 5.4 %all-to-all-start.2 = ((bf16[64,4,896]{2,1,0:T(4,128)(2,1)}), bf16[64,4,896]{2,1,0:T(4,128)(2,1)S(1)}, u32[]{:S(2)}, u32[]{:S(2)}) async-start(bf16[64,4,896]{2,1,0:T(4,128)(2,1)} %get-tuple-element.10), calls=%async_computation.2 | async-start | bytes 917504 | tf_op jit(solution)/shard_map/all_to_all | solution.py:29
  59.0 0.0 copy-done.2
  59.0 0.0 collective-permute-done.2.refs_1_.gate_other
  59.0 0.0 collective-permute-done.3.refs_3_.up_other
  59.0 1.8 %stage.3.staged = bf16[6,896,256]{2,1,0:T(8,128)(2,1)S(1)} custom-call(f32[4,896]{1,0:T(4,128)S(1)} %get-tuple-element.12.after.residual, bf16[7168,256]{1,0:T(8,128)(2,1)} %bitcast.15, bf16[7168,256]{1,0:T(8,128)(2,1)} %collective-permute-done.2.refs_1_.gate_other, bf16[7168,256]{1,0:T(8,128)(2,1)} %bitcast.18, ...), custom_call_target="tpu_custom_call" | custom-call | bytes 5505024 | tf_op jit(solution)/shard_map/stage/pallas_call | solution.py:296
  60.8 9.4 %all-to-all-done.2 = bf16[64,4,896]{2,1,0:T(4,128)(2,1)S(1)} async-done(((bf16[64,4,896]{2,1,0:T(4,128)(2,1)}), bf16[64,4,896]{2,1,0:T(4,128)(2,1)S(1)}, u32[]{:S(2)}, u32[]{:S(2)}) %all-to-all-start.2) | async-done | bytes 458784 | tf_op jit(solution)/shard_map/all_to_all | solution.py:29
  70.2 0.0 collective-permute-done.4.down_other
  70.2 7.6 %experts.1 = bf16[8,8,4,896]{3,2,1,0:T(4,128)(2,1)S(1)} custom-call(bf16[8,8,4,896]{3,2,1,0:T(4,128)(2,1)S(1)} %bitcast.9, f32[8,896]{1,0:T(8,128)S(1)} %reshape.14.gain, f32[2,8,4,128]{3,2,1,0:T(4,128)S(1)} %get-tuple-element.11.coefficients, bf16[6,896,256]{2,1,0:T(8,128)(2,1)S(1)} %stage.3.staged, bf16[7168,256]{1,0:T(8,128)(2,1)} %bitcast.16, ...), custom_call_target="tpu_custom_call" | custom-call | tf_op jit(solution)/shard_map/experts/pallas_call | solution.py:391
  77.8 16.4 %all_to_all.21.arrived = bf16[64,4,896]{2,1,0:T(4,128)(2,1)S(1)} all-to-all(bf16[64,4,896]{2,1,0:T(4,128)(2,1)S(1)} %bitcast.10), channel_id=1, replica_groups=mesh['pair'=8,'core'=2,'dev'=8] {'pair','dev'}, dimensions={0} | all-to-all | bytes 917504 | tf_op jit(solution)/shard_map/all_to_all | solution.py:29
  94.2 0.8 finish.1
  (1 shorter events, 0.0 us)
Async XLA Ops:
  0.0 59.0 %collective-permute-start.2 = (bf16[7168,256]{1,0:T(8,128)(2,1)}, bf16[7168,256]{1,0:T(8,128)(2,1)}, u32[]{:S(2)}, u32[]{:S(2)}) collective-permute-start(bf16[7168,256]{1,0:T(8,128)(2,1)} %bitcast.14), channel_id=1, source_target_pairs={{0,8},{8,0},{1,9},{9,1},{2,10},{10,2},{3,11},{11,3},{4,12},{12,4},... | collective-permute-start | bytes 11010056 | tf_op jit(solution)/shard_map/ppermute | solution.py:33
  0.0 59.0 %collective-permute-start.3 = (bf16[7168,256]{1,0:T(8,128)(2,1)}, bf16[7168,256]{1,0:T(8,128)(2,1)}, u32[]{:S(2)}, u32[]{:S(2)}) collective-permute-start(bf16[7168,256]{1,0:T(8,128)(2,1)} %bitcast.17), channel_id=1, source_target_pairs={{0,8},{8,0},{1,9},{9,1},{2,10},{10,2},{3,11},{11,3},{4,12},{12,4},... | collective-permute-start | bytes 11010056 | tf_op jit(solution)/shard_map/ppermute | solution.py:33
  0.5 69.7 %collective-permute-start.4 = (bf16[256,7168]{1,0:T(8,128)(2,1)}, bf16[256,7168]{1,0:T(8,128)(2,1)}, u32[]{:S(2)}, u32[]{:S(2)}) collective-permute-start(bf16[256,7168]{1,0:T(8,128)(2,1)} %bitcast.21), channel_id=1, source_target_pairs={{0,8},{8,0},{1,9},{9,1},{2,10},{10,2},{3,11},{11,3},{4,12},{12,4},... | collective-permute-start | bytes 11010056 | tf_op jit(solution)/shard_map/ppermute | solution.py:33
  0.5 33.7 %collective-permute-start.1 = (bf16[128,7168]{1,0:T(8,128)(2,1)}, bf16[128,7168]{1,0:T(8,128)(2,1)}, u32[]{:S(2)}, u32[]{:S(2)}) collective-permute-start(bf16[128,7168]{1,0:T(8,128)(2,1)} %refs_0_.1), channel_id=1, source_target_pairs={{0,8},{8,0},{1,9},{9,1},{2,10},{10,2},{3,11},{11,3},{4,12},{12,4},... | collective-permute-start | bytes 5505032 | tf_op jit(solution)/shard_map/ppermute | solution.py:33
  1.0 20.3 %copy-start = (bf16[1,512,128]{2,1,0:T(8,128)(2,1)S(1)}, bf16[1,512,128]{2,1,0:T(8,128)(2,1)}, u32[]{:S(2)}) copy-start(bf16[1,512,128]{2,1,0:T(8,128)(2,1)} %param.16) | copy-start | bytes 393220
  9.8 24.4 %all-to-all-start = ((bf16[64,8,640]{2,1,0:T(8,128)(2,1)}), bf16[64,8,640]{2,1,0:T(8,128)(2,1)S(1)}, u32[]{:S(2)}, u32[]{:S(2)}) async-start(bf16[64,8,640]{2,1,0:T(8,128)(2,1)} %attend.1.after), calls=%async_computation | async-start | bytes 1310720 | tf_op jit(solution)/shard_map/all_to_all | solution.py:29
  21.4 1.6 %collective-permute-start = (bf16[512,128]{1,0:T(8,128)(2,1)S(1)}, bf16[512,128]{1,0:T(8,128)(2,1)S(1)}, u32[]{:S(2)}, u32[]{:S(2)}) collective-permute-start(bf16[512,128]{1,0:T(8,128)(2,1)S(1)} %bitcast.12), channel_id=1, source_target_pairs={{0,8},{8,0},{1,9},{9,1},{2,10},{10,2},{3,11},{11,3},{4,12},{12,4},... | collective-permute-start | bytes 393224 | tf_op jit(solution)/shard_map/ppermute | solution.py:33
  22.9 29.6 %copy-start.1 = (bf16[4,7168]{1,0:T(4,128)(2,1)S(1)}, bf16[4,7168]{1,0:T(4,128)(2,1)}, u32[]{:S(2)}) copy-start(bf16[4,7168]{1,0:T(4,128)(2,1)} %hidden.1) | copy-start | bytes 172036
  22.9 36.0 %copy-start.2 = (f32[7168]{0:T(1024)S(1)}, f32[7168]{0:T(1024)}, u32[]{:S(2)}) copy-start(f32[7168]{0:T(1024)} %param.18) | copy-start | bytes 86020
  53.6 16.6 %all-to-all-start.2 = ((bf16[64,4,896]{2,1,0:T(4,128)(2,1)}), bf16[64,4,896]{2,1,0:T(4,128)(2,1)S(1)}, u32[]{:S(2)}, u32[]{:S(2)}) async-start(bf16[64,4,896]{2,1,0:T(4,128)(2,1)} %get-tuple-element.10), calls=%async_computation.2 | async-start | bytes 917504 | tf_op jit(solution)/shard_map/all_to_all | solution.py:29
